TPU v7x, 32 devices: a whole 2x2x4 slice. The times are simulated.
32 devices in a mesh: rows: 16 (over z, y, core), seq: 2 (over x).
Axes of the slice: x: 2, y: 2, z: 4, core: 2. Of those that a mesh axis runs over, the one named last changes fastest.
Arguments:
- hidden_in: bfloat16 [16, 1280, 512], P('rows', 'seq'), may hold values from -6 to 6
- memory: bfloat16 [16, 256, 512], P('rows', 'seq'), may hold values from -6 to 6
- grad_out: bfloat16 [16, 1280, 512], P('rows', 'seq'), may hold values from -6 to 6
- seg_ids: int32 [16, 1280], P('rows'), may hold values from 0 to 2, as said below
- mem_seg_ids: int32 [16, 256], P('rows'), may hold values from 0 to 2, as said below
- gains: bfloat16 [5, 512], P(None, 'seq'), may hold values from 0.25 to 1.75
- qkv_first: bfloat16 [512, 1536], P('seq'), may hold values from -0.25 to 0.25
- query_cross: bfloat16 [512, 512], P('seq'), may hold values from -0.25 to 0.25
- kv_cross: bfloat16 [512, 1024], P('seq'), may hold values from -0.25 to 0.25
- out_first: bfloat16 [1024, 512], P(None, 'seq'), may hold values from -2 to 2
- taps_left: bfloat16 [11, 512], P(None, 'seq'), may hold values from -1.75 to 1.75
- proj_left: bfloat16 [512, 1024], P('seq'), may hold values from -0.25 to 0.25
- taps_right: bfloat16 [7, 512], P(None, 'seq'), may hold values from -2 to 2
- proj_right: bfloat16 [512, 256], P('seq'), may hold values from -0.25 to 0.25
- mid_gain: bfloat16 [1024], P('seq'), may hold values from 0.25 to 1.75
- taps_mid: bfloat16 [7, 1024], P(None, 'seq'), may hold values from -2 to 2
- proj_mid: bfloat16 [1024, 512], P(None, 'seq'), may hold values from -0.375 to 0.375
- qkv_second: bfloat16 [512, 1536], P('seq'), may hold values from -0.25 to 0.25
- out_second: bfloat16 [512, 512], P('seq'), may hold values from -2 to 2
- query_last: bfloat16 [512, 512], P('seq'), may hold values from -0.25 to 0.25
- kv_last: bfloat16 [512, 1024], P('seq'), may hold values from -0.25 to 0.25
- out_last: bfloat16 [512, 512], P('seq'), may hold values from -2 to 2
- ffn_up: bfloat16 [512, 2048], P('seq'), may hold values from -0.25 to 0.25
- ffn_down: bfloat16 [2048, 512], P(None, 'seq'), may hold values from -0.125 to 0.125
Outputs:
- output: bfloat16 [16, 1280, 512], P('rows', 'seq')
- grad_in: float32 [16, 1280, 512], P('rows', 'seq')
- grad_mem: float32 [16, 256, 512], P('rows', 'seq')
- grad_gains: float32 [5, 512], P(None, 'seq')
- grad_qkv_first: float32 [512, 1536], P('seq')
- grad_query_cross: float32 [512, 512], P('seq')
- grad_kv_cross: float32 [512, 1024], P('seq')
- grad_out_first: float32 [1024, 512], P(None, 'seq')
- grad_taps_left: float32 [11, 512], P(None, 'seq')
- grad_proj_left: float32 [512, 1024], P('seq')
- grad_taps_right: float32 [7, 512], P(None, 'seq')
- grad_proj_right: float32 [512, 256], P('seq')
- grad_mid_gain: float32 [1024], P('seq')
- grad_taps_mid: float32 [7, 1024], P(None, 'seq')
- grad_proj_mid: float32 [1024, 512], P(None, 'seq')
- grad_qkv_second: float32 [512, 1536], P('seq')
- grad_out_second: float32 [512, 512], P('seq')
- grad_query_last: float32 [512, 512], P('seq')
- grad_kv_last: float32 [512, 1024], P('seq')
- grad_out_last: float32 [512, 512], P('seq')
- grad_ffn_up: float32 [512, 2048], P('seq')
- grad_ffn_down: float32 [2048, 512], P(None, 'seq')
Inputs may be any that keep to these rules, and one draw needn't show every extreme that they name: `seg_ids`: in every row the ids never fall along the positions, and 0, 1 and 2 each occur. `mem_seg_ids`: in every row the ids never fall along the positions, and 0, 1 and 2 each occur.
All inputs are finite; a program needn't handle non-finite values.
Results may differ from a plain program's by a relative error of at most 0.02.
Values may be sent and summed in bfloat16 or wider, within the bound.
A program may use at most 320 MiB of HBM per device.

v0:
```python
import functools

import jax
import jax.numpy as jnp
from jax import lax
from jax.experimental import pallas as pl
from jax.experimental.pallas import tpu as pltpu
from jax.sharding import PartitionSpec as P

H_SELF = 16
H_CROSS = 8
WIDE = 1024
NARROW = 256
LEFT_TAPS = 11
RIGHT_TAPS = 7


NEG_BIG = -1e30
EPSILON = 1e-06


def rotated(block, axis, distance):
    size = lax.axis_size(axis)
    return lax.ppermute(block, axis, [((i + distance) % size, i) for i in range(size)])


def core_swapped(block):
    return lax.ppermute(block, "rows", [(i, i ^ 1) for i in range(lax.axis_size("rows"))])


def in_place_order(relative, dim):
    count = len(relative)
    place = lax.axis_index("seq")
    orders = [
        jnp.concatenate([relative[(p - me) % count] for p in range(count)], dim)
        for me in range(count)
    ]
    result = orders[0]
    for me in range(1, count):
        result = jnp.where(place == me, orders[me], result)
    return result


def gathered(block, dim=0):
    count = lax.axis_size("seq")
    return in_place_order([block] + [rotated(block, "seq", d) for d in range(1, count)], dim)


def near_swapped(block):
    return lax.ppermute(block, "rows", [(i, i ^ 2) for i in range(lax.axis_size("rows"))])


def flat_share(shard, dim, index, count):
    size = shard.shape[0] // count
    part = lax.dynamic_slice_in_dim(shard, index * size, size)
    if dim == 0:
        return part
    width = shard.shape[1]
    blocks = part.reshape(-1, width // count, width)
    return jnp.swapaxes(blocks, 0, 1).reshape(width // count, -1)


def unflat_share(part, shape, dim, count):
    if dim == 0:
        return part
    width = shape[1]
    blocks = part.reshape(width // count, -1, width)
    return jnp.swapaxes(blocks, 0, 1).reshape(shape[0] // count, width)


def seq_rotated(packed):
    return [rotated(packed, "seq", d) for d in range(1, lax.axis_size("seq"))]


def packed_half(shards, dims):
    core = lax.axis_index("rows") & 1
    return jnp.concatenate([flat_share(shard, dim, core, 2) for shard, dim in zip(shards, dims)], 1)


def packed_quarter(shards, dims):
    index = lax.axis_index("rows") & 3
    return jnp.concatenate([flat_share(shard, dim, index, 4) for shard, dim in zip(shards, dims)], 1)


def ordered(bit, first, second):
    return jnp.where(bit == 0, jnp.concatenate([first, second], 0), jnp.concatenate([second, first], 0))


def joined_weight(shard, dim, pieces, offset, count):
    row = lax.axis_index("rows")
    size = shard.size // count // pieces[0].shape[0]

    def part(piece):
        return unflat_share(piece[:, offset : offset + size], shard.shape, dim, count)

    relative = [shard]
    if count == 2:
        for k in range(0, len(pieces), 2):
            relative.append(ordered(row & 1, part(pieces[k]), part(pieces[k + 1])))
    else:
        for k in range(0, len(pieces), 3):
            same, near, across = pieces[k : k + 3]
            rows = same.shape[0]
            own_pair = ordered(row & 1, part(same), part(across[:rows]))
            near_pair = ordered(row & 1, part(near), part(across[rows:]))
            relative.append(ordered(row & 2, own_pair, near_pair))
    return in_place_order(relative, dim), offset + size


def joined_group(shards, dims, pieces, count):
    results = []
    offset = 0
    for shard, dim in zip(shards, dims):
        full, offset = joined_weight(shard, dim, pieces, offset, count)
        results.append(full)
    return results


def interleaved(*lists):
    return [item for items in zip(*lists) for item in items]


def small_gather(shards, dims):
    sizes = [shard.size for shard in shards]
    flat = jnp.concatenate([shard.reshape(-1) for shard in shards])
    flat = padded_rows(flat, 2048, 0).reshape(-1, 128)
    parts = [flat] + [rotated(flat, "seq", d) for d in range(1, lax.axis_size("seq"))]
    parts = [part.reshape(-1) for part in parts]
    results = []
    offset = 0
    for shard, dim, size in zip(shards, dims, sizes):
        relative = [part[offset : offset + size].reshape(shard.shape) for part in parts]
        results.append(in_place_order(relative, dim))
        offset = offset + size
    return results


def padded_rows(block, multiple, dim):
    extra = -block.shape[dim] % multiple
    if not extra:
        return block
    widths = [(0, 0)] * block.ndim
    widths[dim] = (0, extra)
    return jnp.pad(block, widths)


def small_rows(grads, width):
    seq_count = lax.axis_size("seq")
    rows = [
        jnp.moveaxis(grad.reshape(-1, seq_count, grad.shape[-1] // (seq_count * width), width), 1, 2).reshape(
            -1, seq_count * width
        )
        for grad in grads
    ]
    return padded_rows(jnp.concatenate(rows, 0), 128, 0)


def small_shares(columns, grads, width):
    seq_count = lax.axis_size("seq")
    rows = columns.T
    results = []
    offset = 0
    for grad in grads:
        count = grad.size // (seq_count * width)
        shape = grad.shape[:-1] + (grad.shape[-1] // seq_count,)
        results.append(rows[offset : offset + count].reshape(shape))
        offset = offset + count
    return results


def halved_sum(block, axis, bit, dim):
    half = block.shape[dim] // 2
    upper = ((lax.axis_index(axis) & bit) != 0).astype(jnp.int32)
    kept = lax.dynamic_slice_in_dim(block, upper * half, half, dim)
    sent = lax.dynamic_slice_in_dim(block, (1 - upper) * half, half, dim)
    got = lax.ppermute(sent, axis, [(i, i ^ bit) for i in range(lax.axis_size(axis))])
    return (kept.astype(jnp.float32) + got.astype(jnp.float32)).astype(jnp.bfloat16)


def row_sum_owned(partial):
    bit = lax.axis_size("seq") // 2
    while bit:
        partial = halved_sum(partial, "seq", bit, 0)
        bit = bit // 2
    return partial.astype(jnp.float32)


def after(values, others):
    return lax.optimization_barrier((values, others))


def passed_along(block, axis, distance):
    devices = range(lax.axis_size(axis))
    route = [(i - distance, i) for i in devices if i - distance in devices]
    return lax.ppermute(block, axis, route)


def layer_norm(values, gain_vec):
    centre = values - jnp.mean(values, axis=-1, keepdims=True)
    inverse = lax.rsqrt(jnp.mean(centre * centre, axis=-1, keepdims=True) + EPSILON)
    return centre * inverse * gain_vec


def norm_back(values, gain_vec, upstream):
    centre = values - jnp.mean(values, axis=-1, keepdims=True)
    inverse = lax.rsqrt(jnp.mean(centre * centre, axis=-1, keepdims=True) + EPSILON)
    normed = centre * inverse
    scaled = upstream * gain_vec
    d_values = inverse * (
        scaled
        - jnp.mean(scaled, axis=-1, keepdims=True)
        - normed * jnp.mean(scaled * normed, axis=-1, keepdims=True)
    )
    return (d_values, jnp.sum(upstream * normed, axis=0))


def swish_slope(pre_act):
    sigma = jax.nn.sigmoid(pre_act)
    return sigma * (1.0 + pre_act * (1.0 - sigma))


def plain_dot(first, second):
    return jnp.dot(first, second, preferred_element_type=jnp.float32)


def left_dot(first, second):
    return jnp.einsum("nk,nm->km", first, second, preferred_element_type=jnp.float32)


def right_dot(grads_in, weight):
    return jnp.einsum("nm,km->nk", grads_in, weight, preferred_element_type=jnp.float32)


TILE = 256
SEG_ROWS = 16
LOG2E = 1.4426950408889634


def tiles_of(extent):
    return [(low, min(low + TILE, extent)) for low in range(0, extent, TILE)]


def tn_dot(first, second):
    return lax.dot_general(first, second, (((0,), (0,)), ((), ())), preferred_element_type=jnp.float32)


def nn_dot(first, second):
    return lax.dot_general(first, second, (((1,), (0,)), ((), ())), preferred_element_type=jnp.float32)


def nt_dot(first, second):
    return lax.dot_general(first, second, (((1,), (1,)), ((), ())), preferred_element_type=jnp.float32)


def row_numbers(width):
    return lax.broadcasted_iota(jnp.int32, (SEG_ROWS, width), 0)


def split_low(values, count):
    pieces = []
    for _ in range(count):
        piece = values.astype(jnp.bfloat16).astype(jnp.float32)
        pieces.append(piece)
        values = values - piece
    return pieces


def key_marks(key_seg, ones):
    rows = row_numbers(key_seg.shape[1])
    marked = jnp.logical_or(rows == key_seg, jnp.logical_and(rows >= 3, rows < 3 + ones))
    return jnp.where(marked, 1.0, 0.0).astype(jnp.bfloat16)


def query_marks(query_seg):
    rows = row_numbers(query_seg.shape[1])
    other = jnp.logical_and(rows < 3, rows != query_seg)
    return jnp.where(other, NEG_BIG, 0.0)


def with_rows(marks, first, pieces):
    rows = row_numbers(marks.shape[1])
    for k, piece in enumerate(pieces):
        marks = jnp.where(rows == first + k, piece, marks)
    return marks.astype(jnp.bfloat16)


def triangle(scores, low):
    key_at = lax.broadcasted_iota(jnp.int32, scores.shape, 0)
    query_at = lax.broadcasted_iota(jnp.int32, scores.shape, 1) + low
    return jnp.where(key_at <= query_at, scores, NEG_BIG)


FWD_HEADS = 4
BWD_HEADS = 4


def attend_kernel(heads, causal, place_ref, *refs):
    attend_core(heads, causal, place_ref[0], *refs)


def attend_core(
    heads, causal, place, qt_ref, pair_ref, qseg_ref, kseg_ref, ot_ref, total_ref, kmark_ref, sum_ref, peak_ref, score_ref
):
    width, tokens = qt_ref.shape
    size = width // heads
    factor = size ** (-0.5) * LOG2E
    block = tokens if causal else pair_ref.shape[1]
    place = place if causal else 0
    kmark_ref[...] = key_marks(kseg_ref[...], 0)
    value_marks = jnp.where(row_numbers(TILE) == 0, 1.0, 0.0).astype(jnp.bfloat16)
    qmarks = query_marks(qseg_ref[...]).astype(jnp.bfloat16)
    tiles = tiles_of(tokens)

    def head_rows(head, base=0):
        return pl.ds(pl.multiple_of(base + head * size, size), size)

    def on_units(several, start, first):
        units = [(k, head, low, high) for k, head in enumerate(several) for low, high in tiles]

        def key_parts(unit):
            _, _, _, high = unit
            return tiles_of(high if first and causal else block)

        def lanes_of(part):
            return pl.ds(pl.multiple_of(start + part[0], 128), part[1] - part[0])

        def score_part(unit, slot, part):
            k, head, low, high = unit
            query_rows = jnp.concatenate([qt_ref[head_rows(head), low:high], qmarks[:, low:high]], 0)
            lanes = lanes_of(part)
            scores = tn_dot(jnp.concatenate([pair_ref[head_rows(head), lanes], kmark_ref[:, lanes]], 0), query_rows)
            if first and causal and part[0] >= low:
                scores = triangle(scores, low - part[0])
            score_ref[slot, part[0] : part[1], : high - low] = scores
            return jnp.max(scores, axis=0, keepdims=True)

        def value_part(unit, slot, part, peak):
            k, head, low, high = unit
            scores = score_ref[slot, part[0] : part[1], : high - low]
            weights = jnp.exp2((scores - peak) * factor).astype(jnp.bfloat16)
            value_rows = jnp.concatenate(
                [pair_ref[head_rows(head, width), lanes_of(part)], value_marks[:, : part[1] - part[0]]], 0
            )
            return nn_dot(value_rows, weights)

        held = None
        for at in range(len(units) + 1):
            unit = units[at] if at < len(units) else None
            parts = key_parts(unit) if unit else []
            old_parts = key_parts(held[0]) if held else []
            peak = None
            if unit and not first:
                peak = peak_ref[unit[0], :, unit[2] : unit[3]]
            before = peak
            summed = None
            for step in range(max(len(parts), len(old_parts))):
                if step < len(parts):
                    found = score_part(unit, at % 2, parts[step])
                    peak = found if peak is None else jnp.maximum(peak, found)
                if step < len(old_parts):
                    term = value_part(held[0], (at - 1) % 2, old_parts[step], held[1])
                    summed = term if summed is None else summed + term
            if held:
                k, _, low, high = held[0]
                if not first:
                    summed = summed + sum_ref[k, :, low:high] * jnp.exp2((held[2] - held[1]) * factor)
                sum_ref[k, :, low:high] = summed
                peak_ref[k, :, low:high] = held[1]
            held = (unit, peak, before)

    def some_heads(step, carry):
        several = [step * FWD_HEADS + k for k in range(FWD_HEADS)]
        on_units(several, place * block, True)
        if causal:

            def earlier(back, held):
                on_units(several, back * block, False)
                return held

            lax.fori_loop(0, place, earlier, 0)
        for k, head in enumerate(several):
            total = sum_ref[k, size : size + 1, :]
            ot_ref[head_rows(head), :] = (sum_ref[k, :size, :] / total).astype(jnp.bfloat16)
            total_ref[head] = peak_ref[k] + jnp.log2(total) / factor
        return carry

    lax.fori_loop(0, heads // FWD_HEADS, some_heads, 0)


def attend_back_kernel(heads, causal, place_ref, *refs):
    attend_back_core(heads, causal, place_ref[0], *refs)


def attend_back_core(
    heads, causal, place, qt_ref, pair_ref, gt_ref, ot_ref, total_ref, qseg_ref, kseg_ref,
    dq_ref, dpair_ref, kmark_ref, dkh_ref, dvh_ref, dqh_ref, qrow_ref, grow_ref, weight_ref, slope_ref,
    pump=None,
):
    width, tokens = qt_ref.shape
    size = width // heads
    scale = size ** (-0.5)
    factor = scale * LOG2E
    block = tokens if causal else pair_ref.shape[1]
    place = place if causal else 0
    kmark_ref[...] = key_marks(kseg_ref[...], 3)
    value_marks = jnp.where(row_numbers(TILE) < 2, 1.0, 0.0).astype(jnp.bfloat16)
    qmarks = query_marks(qseg_ref[...])
    tiles = tiles_of(tokens)

    def head_rows(head, base=0):
        return pl.ds(pl.multiple_of(base + head * size, size), size)

    def prepare(k, head):
        own = head_rows(head)
        grads = gt_ref[own, :]
        delta = jnp.sum(grads.astype(jnp.float32) * ot_ref[own, :].astype(jnp.float32), axis=0, keepdims=True)
        qrow_ref[k, :size, :] = qt_ref[own, :]
        qrow_ref[k, size : size + SEG_ROWS, :] = with_rows(qmarks, 3, split_low(-total_ref[head], 3))
        grow_ref[k, :size, :] = grads
        grow_ref[k, size : size + SEG_ROWS, :] = with_rows(jnp.zeros_like(qmarks), 0, split_low(-delta, 2))

    def on_units(several, start, first):
        units = [(k, head, low, high) for k, head in enumerate(several) for low, high in tiles]

        def key_parts(unit):
            _, _, _, high = unit
            return tiles_of(high if first and causal else block)

        def lanes_of(part):
            return pl.ds(pl.multiple_of(start + part[0], 128), part[1] - part[0])

        def score_part(unit, slot, part):
            k, head, low, high = unit
            lanes = lanes_of(part)
            key_rows = jnp.concatenate([pair_ref[head_rows(head), lanes], kmark_ref[:, lanes]], 0)
            value_rows = jnp.concatenate(
                [pair_ref[head_rows(head, width), lanes], value_marks[:, : part[1] - part[0]]], 0
            )
            scores = tn_dot(key_rows, qrow_ref[k, : size + SEG_ROWS, low:high])
            if first and causal and part[0] >= low:
                scores = triangle(scores, low - part[0])
            weights = jnp.exp2(scores * factor)
            slopes = tn_dot(value_rows, grow_ref[k, : size + SEG_ROWS, low:high])
            weight_ref[slot, part[0] : part[1], : high - low] = weights.astype(jnp.bfloat16)
            slope_ref[slot, part[0] : part[1], : high - low] = (weights * slopes).astype(jnp.bfloat16)

        def grad_part(unit, slot, part):
            k, head, low, high = unit
            lanes = lanes_of(part)
            weights = weight_ref[slot, part[0] : part[1], : high - low]
            slopes = slope_ref[slot, part[0] : part[1], : high - low]
            dvh_ref[k, :, lanes] += nt_dot(grow_ref[k, :size, low:high], weights)
            dkh_ref[k, :, lanes] += nt_dot(qrow_ref[k, :size, low:high], slopes)
            return nn_dot(pair_ref[head_rows(head), lanes], slopes)

        held = None
        for at in range(len(units) + 1):
            unit = units[at] if at < len(units) else None
            parts = key_parts(unit) if unit else []
            old_parts = key_parts(held) if held else []
            summed = None
            for step in range(max(len(parts), len(old_parts))):
                if step < len(parts):
                    score_part(unit, at % 2, parts[step])
                if step < len(old_parts):
                    term = grad_part(held, (at - 1) % 2, old_parts[step])
                    summed = term if summed is None else summed + term
            if held:
                k, _, low, high = held
                if first:
                    dqh_ref[k, :size, low:high] = summed
                else:
                    dqh_ref[k, :size, low:high] += summed
            held = unit

    def some_heads(step, carry):
        several = [step * BWD_HEADS + k for k in range(BWD_HEADS)]
        if pump is not None:
            pump(step)
        dkh_ref[...] = jnp.zeros_like(dkh_ref)
        dvh_ref[...] = jnp.zeros_like(dvh_ref)
        for k, head in enumerate(several):
            prepare(k, head)
        on_units(several, place * block, True)
        if causal:

            def earlier(back, held):
                on_units(several, back * block, False)
                return held

            lax.fori_loop(0, place, earlier, 0)
        for k, head in enumerate(several):
            dq_ref[head_rows(head), :] = (dqh_ref[k, :size, :] * scale).astype(jnp.bfloat16)
            dpair_ref[head_rows(head), :] = (dkh_ref[k] * scale).astype(jnp.bfloat16)
            dpair_ref[head_rows(head, width), :] = dvh_ref[k].astype(jnp.bfloat16)
        return carry

    lax.fori_loop(0, heads // BWD_HEADS, some_heads, 0)


IN_SMEM = pl.BlockSpec(memory_space=pltpu.SMEM)
IN_VMEM = pl.BlockSpec(memory_space=pltpu.VMEM)
KERNEL_VMEM = 48 * 2**20


LANE_GROUP = 128


def attend_forward(queries, pairs_t, heads, causal, query_seg, key_seg):
    width, tokens = queries.shape
    total_keys = pairs_t.shape[1]
    pairs = heads * tokens * total_keys
    return pl.pallas_call(
        functools.partial(attend_kernel, heads, causal),
        out_shape=(
            jax.ShapeDtypeStruct((width, tokens), jnp.bfloat16),
            jax.ShapeDtypeStruct((heads, 1, tokens), jnp.float32),
        ),
        in_specs=[IN_SMEM] + [IN_VMEM] * 4,
        out_specs=(IN_VMEM, IN_VMEM),
        scratch_shapes=[
            pltpu.VMEM((SEG_ROWS, total_keys), jnp.bfloat16),
            pltpu.VMEM((FWD_HEADS, width // heads + SEG_ROWS, tokens), jnp.float32),
            pltpu.VMEM((FWD_HEADS, 1, tokens), jnp.float32),
            pltpu.VMEM((2, tokens if causal else total_keys, TILE), jnp.float32),
        ],
        compiler_params=pltpu.CompilerParams(vmem_limit_bytes=KERNEL_VMEM),
        cost_estimate=pl.CostEstimate(
            flops=pairs * 600, bytes_accessed=4 * width * total_keys, transcendentals=pairs
        ),
        name="attend_fwd",
    )(lax.axis_index("seq").reshape(1), queries, pairs_t, query_seg[None], key_seg[None])


def attend_back(queries, pairs_t, grads, outs, totals, heads, causal, query_seg, key_seg):
    width, tokens = queries.shape
    total_keys = pairs_t.shape[1]
    pairs = heads * tokens * total_keys
    size = width // heads
    return pl.pallas_call(
        functools.partial(attend_back_kernel, heads, causal),
        out_shape=(
            jax.ShapeDtypeStruct((width, tokens), jnp.bfloat16),
            jax.ShapeDtypeStruct((2 * width, total_keys), jnp.bfloat16),
        ),
        in_specs=[IN_SMEM] + [IN_VMEM] * 7,
        out_specs=(IN_VMEM, IN_VMEM),
        scratch_shapes=[
            pltpu.VMEM((SEG_ROWS, total_keys), jnp.bfloat16),
            pltpu.VMEM((BWD_HEADS, size, total_keys), jnp.float32),
            pltpu.VMEM((BWD_HEADS, size, total_keys), jnp.float32),
            pltpu.VMEM((BWD_HEADS, size, tokens), jnp.float32),
            pltpu.VMEM((BWD_HEADS, size + SEG_ROWS, tokens), jnp.bfloat16),
            pltpu.VMEM((BWD_HEADS, size + SEG_ROWS, tokens), jnp.bfloat16),
            pltpu.VMEM((2, tokens if causal else total_keys, TILE), jnp.bfloat16),
            pltpu.VMEM((2, tokens if causal else total_keys, TILE), jnp.bfloat16),
        ],
        compiler_params=pltpu.CompilerParams(vmem_limit_bytes=KERNEL_VMEM),
        cost_estimate=pl.CostEstimate(
            flops=pairs * 1500, bytes_accessed=8 * width * total_keys, transcendentals=pairs
        ),
        name="attend_bwd",
    )(
        lax.axis_index("seq").reshape(1), queries, pairs_t, grads, outs, totals,
        query_seg[None], key_seg[None],
    )


RIM = 16
ROW_TILE = 64
MERGE_ROWS = 64


def row_tiles(extent, tile):
    return [(low, min(low + tile, extent)) for low in range(0, extent, tile)]


def halves_of(extent):
    middle = -(-extent // 32) * 16
    return [(0, middle), (middle, extent)]


def group_lanes(group):
    return pl.ds(pl.multiple_of(group * 128, 128), 128)


def wide_rows(column, width=128):
    return jnp.broadcast_to(column, (column.shape[0], width))


def loop_rows(extent, tile, body):
    def step(k, carry):
        body(pl.ds(pl.multiple_of(k * tile, tile), tile))
        return carry

    whole = extent // tile
    lax.fori_loop(0, whole, step, 0)
    if whole * tile < extent:
        body(pl.ds(whole * tile, extent - whole * tile))


def rows_normed(values):
    centre = values - jnp.mean(values, axis=-1, keepdims=True)
    inverse = lax.rsqrt(jnp.mean(centre * centre, axis=-1, keepdims=True) + EPSILON)
    return centre * inverse, inverse


def rows_norm_back(normed, inverse, gain_vec, upstream):
    scaled = upstream * gain_vec
    return inverse * (
        scaled
        - jnp.mean(scaled, axis=-1, keepdims=True)
        - normed * jnp.mean(scaled * normed, axis=-1, keepdims=True)
    )


def taps_forward(source_ref, first_row, since, lanes, low, high, weights):
    result = None
    for offset, weight in enumerate(weights):
        start = first_row + low - offset
        window = source_ref[start : start + high - low, lanes]
        if offset:
            window = jnp.where(since >= offset, window, 0.0)
        term = window * weight
        result = term if result is None else result + term
    return result


def conv_fwd_kernel(
    h1_ref, a2_ref, rim_ref, since_ref, tl_ref, tr_ref, tm_ref, mgain_ref, gain_ref, pl_ref, pr_ref, pm_ref,
    cl_ref, cr_ref, cm_ref, h2_ref, a3_ref,
    ext_ref, wide_ref, cle_ref, cre_ref, up_ref, mixed_ref,
):
    tokens, width = h1_ref.shape
    total = tokens + RIM
    narrow = pr_ref.shape[1]
    ext_ref[0:RIM, :] = jnp.zeros((RIM, width), jnp.float32)
    ext_ref[RIM : 2 * RIM, :] = rim_ref[...].astype(jnp.float32)
    ext_ref[2 * RIM :, :] = a2_ref[...].astype(jnp.float32)
    wide_ref[...] = wide_rows(since_ref[...])

    def first_convs(group, carry):
        lanes = group_lanes(group)
        left = [tl_ref[j : j + 1, lanes] for j in range(tl_ref.shape[0])]
        right = [tr_ref[j : j + 1, lanes] for j in range(tr_ref.shape[0])]
        for low, high in row_tiles(total, ROW_TILE):
            since = wide_ref[low:high, :]
            cle_ref[low:high, lanes] = taps_forward(ext_ref, RIM, since, lanes, low, high, left).astype(jnp.bfloat16)
            cre_ref[low:high, lanes] = taps_forward(ext_ref, RIM, since, lanes, low, high, right).astype(jnp.bfloat16)
        return carry

    lax.fori_loop(0, width // 128, first_convs, 0)
    cl_ref[...] = cle_ref[RIM:, :]
    cr_ref[...] = cre_ref[RIM:, :]
    for low, high in halves_of(total):
        up_ref[low:high, :] = nn_dot(cle_ref[low:high, :], pl_ref[...])
        mixed_ref[low:high, :narrow] = nn_dot(cre_ref[low:high, :], pr_ref[...])

    def merge_rows(rows):
        pre = up_ref[rows, :]
        merged = pre / (1.0 + jnp.exp(-pre))
        merged = jnp.concatenate([merged[:, :narrow] + mixed_ref[rows, :narrow], merged[:, narrow:]], 1)
        normed, _ = rows_normed(merged)
        mixed_ref[rows, :] = (normed * mgain_ref[...]).astype(jnp.bfloat16).astype(jnp.float32)

    loop_rows(total, MERGE_ROWS, merge_rows)

    def mid_conv(group, carry):
        lanes = group_lanes(group)
        weights = [tm_ref[j : j + 1, lanes] for j in range(tm_ref.shape[0])]
        for low, high in row_tiles(tokens, ROW_TILE):
            since = wide_ref[RIM + low : RIM + high, :]
            cm_ref[low:high, lanes] = taps_forward(mixed_ref, RIM, since, lanes, low, high, weights).astype(jnp.bfloat16)
        return carry

    lax.fori_loop(0, mixed_ref.shape[1] // 128, mid_conv, 0)
    for low, high in halves_of(tokens):
        h2_ref[low:high, :] = h1_ref[low:high, :] + nn_dot(cm_ref[low:high, :], pm_ref[...])

    def norm_rows(rows):
        normed, _ = rows_normed(h2_ref[rows, :])
        a3_ref[rows, :] = (normed * gain_ref[...]).astype(jnp.bfloat16)

    loop_rows(tokens, 64, norm_rows)


def conv_forward(h1, a2, rim, since, taps_l, taps_r, taps_m, mid_gain, gain, proj_left, proj_right, proj_mid):
    tokens, width = h1.shape
    wide = proj_left.shape[1]
    total = tokens + RIM
    low, full = jnp.bfloat16, jnp.float32
    return pl.pallas_call(
        conv_fwd_kernel,
        out_shape=(
            jax.ShapeDtypeStruct((tokens, width), low),
            jax.ShapeDtypeStruct((tokens, width), low),
            jax.ShapeDtypeStruct((tokens, wide), low),
            jax.ShapeDtypeStruct((tokens, width), full),
            jax.ShapeDtypeStruct((tokens, width), low),
        ),
        in_specs=[IN_VMEM] * 12,
        out_specs=(IN_VMEM,) * 5,
        scratch_shapes=[
            pltpu.VMEM((total + RIM, width), full),
            pltpu.VMEM((total, 128), jnp.int32),
            pltpu.VMEM((total, width), low),
            pltpu.VMEM((total, width), low),
            pltpu.VMEM((total, wide), full),
            pltpu.VMEM((total, wide), full),
        ],
        compiler_params=pltpu.CompilerParams(vmem_limit_bytes=KERNEL_VMEM),
        cost_estimate=pl.CostEstimate(
            flops=tokens * width * wide * 20, bytes_accessed=tokens * width * 16, transcendentals=tokens * wide
        ),
        name="conv_fwd",
    )(h1, a2, rim, since, taps_l, taps_r, taps_m, mid_gain, gain, proj_left, proj_right, proj_mid)


def folded(values):
    return jnp.sum(values.reshape(-1, 8, values.shape[-1]), axis=0)


def taps_back(grad_ref, value, left, lanes, low, high, weights, result, sums):
    for offset, weight in enumerate(weights):
        window = grad_ref[low + offset : high + offset, lanes]
        if offset:
            window = jnp.where(left >= offset, window, 0.0)
        term = window * weight
        result = term if result is None else result + term
        if value is not None:
            product = folded(window * value)
            sums[offset] = product if sums[offset] is None else sums[offset] + product
    return result


def conv_bwd_kernel(
    g2_ref, brim_ref, cl_ref, clrim_ref, cr_ref, crrim_ref, cm_ref, a2_ref, h1_ref, left_ref,
    tl_ref, tr_ref, tm_ref, mgain_ref, gain_ref, pl_ref, pr_ref, pm_ref,
    g1_ref, dw_ref, dtl_ref, dtr_ref, dtm_ref, dmgain_ref, dgain_ref,
    bext_ref, cle_ref, cre_ref, wide_ref, grad_ref, up_ref, back_ref, normed_ref, inv_ref, dpl_ref, dpr_ref, a2f_ref,
):
    tokens, width = g2_ref.shape
    total = tokens + RIM
    wide, narrow = pl_ref.shape[1], pr_ref.shape[1]
    bext_ref[:tokens, :] = g2_ref[...].astype(jnp.bfloat16)
    bext_ref[tokens:, :] = brim_ref[...]
    cle_ref[:tokens, :] = cl_ref[...]
    cle_ref[tokens:, :] = clrim_ref[...]
    cre_ref[:tokens, :] = cr_ref[...]
    cre_ref[tokens:, :] = crrim_ref[...]
    a2f_ref[...] = a2_ref[...].astype(jnp.float32)
    wide_ref[...] = wide_rows(left_ref[...])
    grad_ref[total:, :] = jnp.zeros((RIM, wide), jnp.float32)
    dw_ref[:, :wide] = tn_dot(bext_ref[:tokens, :], cm_ref[...]).astype(jnp.bfloat16)
    for low, high in halves_of(total):
        grad_ref[low:high, :] = nt_dot(bext_ref[low:high, :], pm_ref[...])
        up_ref[low:high, :] = nn_dot(cle_ref[low:high, :], pl_ref[...])
        back_ref[low:high, :narrow] = nn_dot(cre_ref[low:high, :], pr_ref[...])

    def merge_rows(rows):
        pre = up_ref[rows, :]
        merged = pre / (1.0 + jnp.exp(-pre))
        merged = jnp.concatenate([merged[:, :narrow] + back_ref[rows, :narrow], merged[:, narrow:]], 1)
        normed, inverse = rows_normed(merged)
        normed_ref[rows, :] = normed
        inv_ref[rows, :] = wide_rows(inverse)

    loop_rows(total, MERGE_ROWS, merge_rows)

    def mid_back(group, carry):
        lanes = group_lanes(group)
        weights = [tm_ref[j : j + 1, lanes] for j in range(tm_ref.shape[0])]
        sums = [None] * len(weights)
        gain_vec = mgain_ref[:, lanes]
        for low, high in row_tiles(total, ROW_TILE):
            value = None
            if high <= tokens:
                value = (normed_ref[low:high, lanes] * gain_vec).astype(jnp.bfloat16).astype(jnp.float32)
            back_ref[low:high, lanes] = taps_back(
                grad_ref, value, wide_ref[low:high, :], lanes, low, high, weights, None, sums
            )
        for j, piece in enumerate(sums):
            dtm_ref[j : j + 1, lanes] = jnp.sum(piece, axis=0, keepdims=True)
        return carry

    lax.fori_loop(0, wide // 128, mid_back, 0)

    def merge_back(rows):
        pre = up_ref[rows, :]
        normed = normed_ref[rows, :]
        d_merged = rows_norm_back(normed, inv_ref[rows, :][:, :1], mgain_ref[...], back_ref[rows, :])
        sigma = 1.0 / (1.0 + jnp.exp(-pre))
        dpl_ref[rows, :] = (d_merged * (sigma * (1.0 + pre * (1.0 - sigma)))).astype(jnp.bfloat16)
        dpr_ref[rows, :] = d_merged[:, :narrow].astype(jnp.bfloat16)

    loop_rows(total, MERGE_ROWS, merge_back)
    gain_sum = jnp.zeros((8, wide), jnp.float32)

    def gain_rows(k, held):
        rows = pl.ds(pl.multiple_of(k * 16, 16), 16)
        return held + folded(back_ref[rows, :] * normed_ref[rows, :])

    gain_sum = lax.fori_loop(0, tokens // 16, gain_rows, gain_sum)
    dmgain_ref[...] = jnp.sum(gain_sum, axis=0, keepdims=True)
    dw_ref[:, wide : 2 * wide] = tn_dot(cle_ref[:tokens, :], dpl_ref[:tokens, :]).astype(jnp.bfloat16)
    dw_ref[:, 2 * wide :] = tn_dot(cre_ref[:tokens, :], dpr_ref[:tokens, :]).astype(jnp.bfloat16)
    for low, high in halves_of(total):
        grad_ref[low:high, :width] = nt_dot(dpl_ref[low:high, :], pl_ref[...])
        grad_ref[low:high, width : 2 * width] = nt_dot(dpr_ref[low:high, :], pr_ref[...])

    def first_back(group, carry):
        lanes = group_lanes(group)
        other = group_lanes(group + width // 128)
        weights_l = [tl_ref[j : j + 1, lanes] for j in range(tl_ref.shape[0])]
        weights_r = [tr_ref[j : j + 1, lanes] for j in range(tr_ref.shape[0])]
        sums_l = [None] * len(weights_l)
        sums_r = [None] * len(weights_r)
        for low, high in row_tiles(tokens, ROW_TILE):
            left = wide_ref[low:high, :]
            value = a2f_ref[low:high, lanes]
            held = taps_back(grad_ref, value, left, lanes, low, high, weights_l, None, sums_l)
            held = taps_back(grad_ref, value, left, other, low, high, weights_r, held, sums_r)
            back_ref[low:high, lanes] = held
        for j, piece in enumerate(sums_l):
            dtl_ref[j : j + 1, lanes] = jnp.sum(piece, axis=0, keepdims=True)
        for j, piece in enumerate(sums_r):
            dtr_ref[j : j + 1, lanes] = jnp.sum(piece, axis=0, keepdims=True)
        return carry

    lax.fori_loop(0, width // 128, first_back, 0)

    def finish(k, held):
        rows = pl.ds(pl.multiple_of(k * 64, 64), 64)
        normed, inverse = rows_normed(h1_ref[rows, :])
        upstream = back_ref[rows, :width]
        g1_ref[rows, :] = g2_ref[rows, :] + rows_norm_back(normed, inverse, gain_ref[...], upstream)
        return held + folded(upstream * normed)

    gain_sum = lax.fori_loop(0, tokens // 64, finish, jnp.zeros((8, width), jnp.float32))
    dgain_ref[...] = jnp.sum(gain_sum, axis=0, keepdims=True)


def conv_back(
    g2, brim, c_l, c_r, rims, c_m, a2, h1, left, taps_l, taps_r, taps_m, mid_gain, gain, proj_left, proj_right, proj_mid
):
    tokens, width = g2.shape
    wide, narrow = proj_left.shape[1], proj_right.shape[1]
    total = tokens + RIM
    low, full = jnp.bfloat16, jnp.float32
    return pl.pallas_call(
        conv_bwd_kernel,
        out_shape=(
            jax.ShapeDtypeStruct((tokens, width), full),
            jax.ShapeDtypeStruct((width, 2 * wide + narrow), low),
            jax.ShapeDtypeStruct(taps_l.shape, full),
            jax.ShapeDtypeStruct(taps_r.shape, full),
            jax.ShapeDtypeStruct(taps_m.shape, full),
            jax.ShapeDtypeStruct((1, wide), full),
            jax.ShapeDtypeStruct((1, width), full),
        ),
        in_specs=[IN_VMEM] * 18,
        out_specs=(IN_VMEM,) * 7,
        scratch_shapes=[
            pltpu.VMEM((total, width), low),
            pltpu.VMEM((total, width), low),
            pltpu.VMEM((total, width), low),
            pltpu.VMEM((total, 128), jnp.int32),
            pltpu.VMEM((total + RIM, wide), full),
            pltpu.VMEM((total, wide), full),
            pltpu.VMEM((total, wide), full),
            pltpu.VMEM((total, wide), full),
            pltpu.VMEM((total, 128), full),
            pltpu.VMEM((total, wide), low),
            pltpu.VMEM((total, narrow), low),
            pltpu.VMEM((tokens, width), full),
        ],
        compiler_params=pltpu.CompilerParams(vmem_limit_bytes=KERNEL_VMEM),
        cost_estimate=pl.CostEstimate(
            flops=tokens * width * wide * 40, bytes_accessed=tokens * width * 40, transcendentals=tokens * wide
        ),
        name="conv_bwd",
    )(
        g2, brim, c_l, rims[:, :width], c_r, rims[:, width:], c_m, a2, h1, left,
        taps_l, taps_r, taps_m, mid_gain, gain, proj_left, proj_right, proj_mid,
    )


MIDDLE_VMEM = 60 * 2**20
DOT_ROWS = 256


def load_weight(copies, sems, target_ref, own_ref, pieces, offset, place, near, core):
    width, size = own_ref.shape
    quarter = width // 4
    count = len(pieces) // 3 + 1
    columns = slice(offset, offset + size)
    parts = [(own_ref, place * width, width)]
    for d in range(1, count):
        source = lax.rem(place + d, count) * width
        same, close, across = pieces[3 * d - 3 : 3 * d]
        parts.append((same.at[:, columns], source + (2 * near + core) * quarter, quarter))
        parts.append((close.at[:, columns], source + (2 - 2 * near + core) * quarter, quarter))
        parts.append((across.at[:quarter, columns], source + (2 * near + 1 - core) * quarter, quarter))
        parts.append((across.at[quarter:, columns], source + (3 - 2 * near - core) * quarter, quarter))
    for source_ref, start, rows in parts:
        copy = pltpu.make_async_copy(
            source_ref, target_ref.at[pl.ds(pl.multiple_of(start, quarter), rows), :], sems.at[len(copies)]
        )
        copy.start()
        copies.append(copy)
    return offset + size


def wait_for(copies):
    for copy in copies:
        copy.wait()


def norm_into(target_ref, source_ref, gain_vec):
    def body(rows):
        normed, _ = rows_normed(source_ref[rows, :])
        target_ref[rows, :] = (normed * gain_vec).astype(jnp.bfloat16)

    loop_rows(source_ref.shape[0], 64, body)


def norm_back_into(target_ref, base_ref, source_ref, gain_vec, upstream_ref):
    def body(k, held):
        rows = pl.ds(pl.multiple_of(k * 64, 64), 64)
        normed, inverse = rows_normed(source_ref[rows, :])
        upstream = upstream_ref[rows, :]
        target_ref[rows, :] = base_ref[rows, :].astype(jnp.float32) + rows_norm_back(
            normed, inverse, gain_vec, upstream
        )
        return held + folded(upstream * normed)

    held = jnp.zeros((8, source_ref.shape[1]), jnp.float32)
    return jnp.sum(lax.fori_loop(0, source_ref.shape[0] // 64, body, held), axis=0, keepdims=True)


def chunks(extent):
    return row_tiles(extent, DOT_ROWS)


def project_into(target_ref, weight_ref, turned_ref, low, high):
    for start, stop in chunks(high - low):
        target_ref[start:stop, :] = tn_dot(weight_ref[:, low + start : low + stop], turned_ref[...]).astype(jnp.bfloat16)


def store_grad(target_ref, start, values):
    target_ref[:, start : start + values.shape[1]] = values.astype(jnp.bfloat16)


def middle_kernel(
    piece_count,
    place_ref, h2_ref, a3_ref, a3more_ref, mem_ref, gout_ref, gain_ref, qseg_ref, kseg_ref, mseg_ref, down_ref,
    qkv_own, out2_own, query_own, kv_own, out_own, up_own, *rest,
):
    pieces, rest = rest[:piece_count], rest[piece_count:]
    (
        result_ref, g3_ref, da3_ref, dw_ref, dgain_ref, dmem_ref,
        wqkv_ref, wout2_ref, wquery_ref, wkv_ref, wout_ref, wup_ref, sems,
        turned_ref, memt_ref, a4_ref, a4t_ref, qt_ref, pair_ref, attc_ref, totalc_ref,
        qdt_ref, paird_ref, attd_ref, totald_ref, h3_ref, h4_ref, act_ref, dup_ref, low_ref, gt_ref, dq_ref, dpair_ref, dpaird_ref,
        back_ref, wide_ref, kmark_ref, mmark_ref, sum_ref, peak_ref, score_ref,
        dkh_ref, dvh_ref, dkm_ref, dvm_ref, dqh_ref, qrow_ref, grow_ref, weight_ref, slope_ref,
    ) = rest
    tokens, width = h2_ref.shape
    place, near, core = place_ref[0], place_ref[1], place_ref[2]
    seq_count = piece_count // 3 + 1
    high_width = wup_ref.shape[1]
    first, copies = [], []
    offset = load_weight(first, sems.at[0], wqkv_ref, qkv_own, pieces, 0, place, near, core)
    for target, own in ((wout2_ref, out2_own), (wquery_ref, query_own), (wkv_ref, kv_own), (wout_ref, out_own)):
        offset = load_weight(copies, sems.at[1], target, own, pieces, offset, place, near, core)
    load_weight(copies, sems.at[1], wup_ref, up_own, pieces, offset, place, near, core)

    own = pl.ds(pl.multiple_of(place * tokens, 128), tokens)
    turned_ref[:, own] = a3_ref[...].T
    for d in range(1, seq_count):
        there = pl.ds(pl.multiple_of(lax.rem(place + d, seq_count) * tokens, 128), tokens)
        turned_ref[:, there] = a3more_ref[d - 1].T
    memt_ref[...] = mem_ref[...].T
    wait_for(first)
    project_into(qt_ref, wqkv_ref, turned_ref.at[:, own], 0, width)
    project_into(pair_ref, wqkv_ref, turned_ref, width, 3 * width)
    attend_core(
        H_CROSS, True, place, qt_ref, pair_ref, qseg_ref, kseg_ref, attc_ref, totalc_ref, kmark_ref, sum_ref, peak_ref, score_ref
    )
    wait_for(copies)
    for low, high in chunks(tokens):
        h3_ref[low:high, :] = h2_ref[low:high, :] + tn_dot(attc_ref[:, low:high], wout2_ref[...])
    norm_into(a4_ref, h3_ref, gain_ref[0:1, :])
    a4t_ref[...] = a4_ref[...].T
    project_into(qdt_ref, wquery_ref, a4t_ref, 0, width)
    project_into(paird_ref, wkv_ref, memt_ref, 0, 2 * width)
    attend_core(
        H_CROSS, False, 0, qdt_ref, paird_ref, qseg_ref, mseg_ref, attd_ref, totald_ref, mmark_ref, sum_ref, peak_ref, score_ref
    )
    for low, high in chunks(tokens):
        h4_ref[low:high, :] = h3_ref[low:high, :] + tn_dot(attd_ref[:, low:high], wout_ref[...])
    norm_into(a4_ref, h4_ref, gain_ref[1:2, :])

    for left, right in row_tiles(high_width, 512):
        for low, high in chunks(tokens):
            pre = nn_dot(a4_ref[low:high, :], wup_ref[:, left:right])
            sigma = 1.0 / (1.0 + jnp.exp(-pre))
            act_ref[low:high, left:right] = (pre * sigma).astype(jnp.bfloat16)
            slope = nt_dot(gout_ref[low:high, :], down_ref[left:right, :])
            dup_ref[low:high, left:right] = (slope * (sigma * (1.0 + pre * (1.0 - sigma)))).astype(jnp.bfloat16)
    for low, high in chunks(tokens):
        result_ref[low:high, :] = (h4_ref[low:high, :] + nn_dot(act_ref[low:high, :], down_ref[...])).astype(jnp.bfloat16)
        back_ref[low:high, :] = nt_dot(dup_ref[low:high, :], wup_ref[...])
    for left, right in row_tiles(high_width, 512):
        store_grad(dw_ref, left, tn_dot(a4_ref[...], dup_ref[:, left:right]))
        store_grad(dw_ref, high_width + left, tn_dot(gout_ref[...], act_ref[:, left:right]))

    at = 2 * high_width
    dgain_ref[1:2, :] = norm_back_into(h4_ref, gout_ref, h4_ref, gain_ref[1:2, :], back_ref)
    low_ref[...] = h4_ref[...].astype(jnp.bfloat16)
    store_grad(dw_ref, at, nn_dot(attd_ref[...], low_ref[...]))
    gt_ref[...] = nt_dot(wout_ref[...], low_ref[...]).astype(jnp.bfloat16)
    attend_back_core(
        H_CROSS, False, 0, qdt_ref, paird_ref, gt_ref, attd_ref, totald_ref, qseg_ref, mseg_ref,
        dq_ref, dpaird_ref, mmark_ref, dkm_ref, dvm_ref, dqh_ref, qrow_ref, grow_ref, weight_ref, slope_ref,
    )
    store_grad(dw_ref, at + width, nt_dot(a4t_ref[...], dq_ref[...]))
    store_grad(dw_ref, at + 2 * width, nt_dot(memt_ref[...], dpaird_ref[...]))
    dmem_ref[...] = nn_dot(wkv_ref[...], dpaird_ref[...]).astype(jnp.bfloat16)
    back_ref[...] = nn_dot(wquery_ref[...], dq_ref[...]).T
    dgain_ref[0:1, :] = norm_back_into(g3_ref, h4_ref, h3_ref, gain_ref[0:1, :], back_ref)
    low_ref[...] = g3_ref[...].astype(jnp.bfloat16)
    at = at + 4 * width
    store_grad(dw_ref, at + 3 * width, nn_dot(attc_ref[...], low_ref[...]))
    gt_ref[...] = nt_dot(wout2_ref[...], low_ref[...]).astype(jnp.bfloat16)
    attend_back_core(
        H_CROSS, True, place, qt_ref, pair_ref, gt_ref, attc_ref, totalc_ref, qseg_ref, kseg_ref,
        dq_ref, dpair_ref, kmark_ref, dkh_ref, dvh_ref, dqh_ref, qrow_ref, grow_ref, weight_ref, slope_ref,
    )
    store_grad(dw_ref, at, nt_dot(turned_ref[:, own], dq_ref[...]))
    for low, high in chunks(2 * width):
        store_grad(dw_ref, at + width + low, nt_dot(turned_ref[...], dpair_ref[low:high, :]))
    for low, high in chunks(width):
        wide_ref[low:high, :] = nn_dot(wqkv_ref[low:high, width:], dpair_ref[...])
        wide_ref[low:high, own] += nn_dot(wqkv_ref[low:high, :width], dq_ref[...])
    for low, high in row_tiles(wide_ref.shape[1], tokens):
        da3_ref[low:high, :] = wide_ref[:, low:high].T.astype(jnp.bfloat16)


def middle(h2, a3, a3_more, mem_rows, grad_out, gains, own_seg, seg_row, mem_seg, down, owns, pieces):
    tokens, width = h2.shape
    keys, mems = seg_row.shape[0], mem_seg.shape[0]
    high_width = down.shape[0]
    seq_count = keys // tokens
    size = width // H_CROSS
    low, full = jnp.bfloat16, jnp.float32
    longest = max(tokens, mems)
    v = pltpu.VMEM
    in_hbm = pl.BlockSpec(memory_space=pl.ANY)
    row = lax.axis_index("rows")
    places = jnp.stack([lax.axis_index("seq"), (row // 2) % 2, row % 2]).astype(jnp.int32)
    return pl.pallas_call(
        functools.partial(middle_kernel, len(pieces)),
        out_shape=(
            jax.ShapeDtypeStruct((tokens, width), low),
            jax.ShapeDtypeStruct((tokens, width), full),
            jax.ShapeDtypeStruct((keys, width), low),
            jax.ShapeDtypeStruct((width, 2 * high_width + 8 * width), low),
            jax.ShapeDtypeStruct((2, width), full),
            jax.ShapeDtypeStruct((width, mems), low),
        ),
        in_specs=[IN_SMEM] + [IN_VMEM] * 10 + [in_hbm] * (6 + len(pieces)),
        out_specs=(IN_VMEM,) * 6,
        scratch_shapes=[
            v((width, 3 * width), low),
            v((width, width), low),
            v((width, width), low),
            v((width, 2 * width), low),
            v((width, width), low),
            v((width, high_width), low),
            pltpu.SemaphoreType.DMA((2, 5 * (4 * seq_count - 3))),
            v((width, keys), low),
            v((width, mems), low),
            v((tokens, width), low),
            v((width, tokens), low),
            v((width, tokens), low),
            v((2 * width, keys), low),
            v((width, tokens), low),
            v((H_CROSS, 1, tokens), full),
            v((width, tokens), low),
            v((2 * width, mems), low),
            v((width, tokens), low),
            v((H_CROSS, 1, tokens), full),
            v((tokens, width), full),
            v((tokens, width), full),
            v((tokens, high_width), low),
            v((tokens, high_width), low),
            v((tokens, width), low),
            v((width, tokens), low),
            v((width, tokens), low),
            v((2 * width, keys), low),
            v((2 * width, mems), low),
            v((tokens, width), full),
            v((width, keys), full),
            v((SEG_ROWS, keys), low),
            v((SEG_ROWS, mems), low),
            v((FWD_HEADS, size + SEG_ROWS, tokens), full),
            v((FWD_HEADS, 1, tokens), full),
            v((2, longest, TILE), full),
            v((BWD_HEADS, size, keys), full),
            v((BWD_HEADS, size, keys), full),
            v((BWD_HEADS, size, mems), full),
            v((BWD_HEADS, size, mems), full),
            v((BWD_HEADS, size, tokens), full),
            v((BWD_HEADS, size + SEG_ROWS, tokens), low),
            v((BWD_HEADS, size + SEG_ROWS, tokens), low),
            v((2, longest, TILE), low),
            v((2, longest, TILE), low),
        ],
        compiler_params=pltpu.CompilerParams(vmem_limit_bytes=MIDDLE_VMEM),
        cost_estimate=pl.CostEstimate(
            flops=tokens * width * width * 200, bytes_accessed=tokens * width * 40, transcendentals=tokens * width * 20
        ),
        name="middle",
    )(
        places, h2, a3, a3_more, mem_rows, grad_out, gains, own_seg[None], seg_row[None], mem_seg[None], down,
        *owns, *pieces,
    )


HOST_VMEM = 63 * 2**20 + 2**19


class ShareSum:
    def __init__(self, seq_count, half, total, out_ref, core_ref, across_ref, close_ref, piece_ref, mine_ref, sems):
        self.seq_count, self.half, self.total = seq_count, half, total
        self.out_ref, self.core_ref, self.across_ref = out_ref, core_ref, across_ref
        self.close_ref, self.piece_ref, self.mine_ref = close_ref, piece_ref, mine_ref
        self.send_sem, self.recv_sem, self.local_sem = sems
        self.far_count = lax.axis_size("rows") // 4
        row, place = lax.axis_index("rows"), lax.axis_index("seq")
        self.core, self.near, self.far, self.place = lax.rem(row, 2), lax.rem(row // 2, 2), row // 4, place
        self.mate = (row + 1 - 2 * self.core, place)
        self.close = (row + 2 - 4 * self.near, place)
        self.peers = [None] + [
            (lax.rem(self.far + d, self.far_count) * 4 + self.near * 2 + self.core, place)
            for d in range(1, self.far_count)
        ]
        self.sides = [None] + [(row, lax.rem(place + d, seq_count)) for d in range(1, seq_count)]
        self.step = 2 * self.far_count * LANE_GROUP
        self.wide = self.far_count * LANE_GROUP
        self.count = total // self.step

    def enter(self):
        barrier = pltpu.get_barrier_semaphore()
        friends = [self.mate, self.close] + self.peers[1:] + self.sides[1:]
        for friend in friends:
            pl.semaphore_signal(barrier, inc=1, device_id=friend, device_id_type=pl.DeviceIdType.MESH)
        pl.semaphore_wait(barrier, len(friends))

    def columns(self, chunk):
        return pl.ds(pl.multiple_of(chunk * self.step, LANE_GROUP), self.step)

    def copy(self, chunk, slot, source, target, device):
        return pltpu.make_async_remote_copy(
            src_ref=source,
            dst_ref=target,
            send_sem=self.send_sem.at[chunk, slot],
            recv_sem=self.recv_sem.at[chunk, slot],
            device_id=device,
            device_id_type=pl.DeviceIdType.MESH,
        )

    def core_copy(self, chunk, source_ref, at):
        return self.copy(chunk, 0, source_ref.at[:, 1 - self.core, :, self.columns(at)], self.core_ref.at[chunk], self.mate)

    def side_copy(self, chunk, d):
        away = lax.rem(self.place + d, self.seq_count)
        return self.copy(chunk, d, self.core_ref.at[chunk, away], self.across_ref.at[chunk, d - 1], self.sides[d])

    def near_copy(self, chunk):
        lanes = pl.ds(pl.multiple_of((1 - self.near) * self.wide, LANE_GROUP), self.wide)
        return self.copy(
            chunk, self.seq_count, self.across_ref.at[chunk, 0, :, lanes], self.close_ref.at[chunk], self.close
        )

    def peer_copy(self, chunk, d):
        away = lax.rem(self.far + d, self.far_count)
        lanes = pl.ds(pl.multiple_of(away * LANE_GROUP, LANE_GROUP), LANE_GROUP)
        return self.copy(
            chunk, self.seq_count + d, self.close_ref.at[chunk, :, lanes], self.piece_ref.at[chunk, d - 1], self.peers[d]
        )

    def own_lanes(self, chunk):
        start = chunk * self.step + self.near * self.wide + self.far * LANE_GROUP
        return pl.ds(pl.multiple_of(start, LANE_GROUP), LANE_GROUP)

    def keep_copy(self, chunk):
        return pltpu.make_async_copy(
            self.mine_ref.at[chunk], self.out_ref.at[self.core, :, self.own_lanes(chunk)], self.local_sem.at[chunk]
        )

    def back_copy(self, chunk, d):
        return self.copy(
            chunk,
            self.seq_count + self.far_count - 1 + d,
            self.mine_ref.at[chunk],
            self.out_ref.at[self.core, :, self.own_lanes(chunk)],
            self.peers[d],
        )

    def near_back(self, chunk):
        start = pl.multiple_of(chunk * self.step + self.near * self.wide, LANE_GROUP)
        block = self.out_ref.at[self.core, :, pl.ds(start, self.wide)]
        return self.copy(chunk, self.seq_count + 2 * self.far_count - 1, block, block, self.close)

    def last_copy(self, chunk):
        block = self.out_ref.at[self.core, :, self.columns(chunk)]
        return self.copy(chunk, self.seq_count + 2 * self.far_count, block, block, self.mate)

    def run_side(self, chunk, kept):
        self.core_ref[chunk] = (kept.astype(jnp.float32) + self.core_ref[chunk].astype(jnp.float32)).astype(jnp.bfloat16)
        for d in range(1, self.seq_count):
            self.side_copy(chunk, d).start()

    def run_near(self, chunk):
        for d in range(1, self.seq_count):
            self.side_copy(chunk, d).wait_recv()
        summed = self.core_ref[chunk, self.place].astype(jnp.float32)
        for d in range(1, self.seq_count):
            summed = summed + self.across_ref[chunk, d - 1].astype(jnp.float32)
        self.across_ref[chunk, 0] = summed.astype(jnp.bfloat16)
        self.near_copy(chunk).start()

    def run_peer(self, chunk):
        self.near_copy(chunk).wait_recv()
        lanes = pl.ds(pl.multiple_of(self.near * self.wide, LANE_GROUP), self.wide)
        summed = self.across_ref[chunk, 0, :, lanes].astype(jnp.float32) + self.close_ref[chunk].astype(jnp.float32)
        self.close_ref[chunk] = summed.astype(jnp.bfloat16)
        for d in range(1, self.far_count):
            self.peer_copy(chunk, d).start()

    def run_back(self, chunk):
        for d in range(1, self.far_count):
            self.peer_copy(chunk, d).wait_recv()
        lanes = pl.ds(pl.multiple_of(self.far * LANE_GROUP, LANE_GROUP), LANE_GROUP)
        summed = self.close_ref[chunk, :, lanes].astype(jnp.float32)
        for d in range(1, self.far_count):
            summed = summed + self.piece_ref[chunk, d - 1].astype(jnp.float32)
        self.mine_ref[chunk] = summed.astype(jnp.bfloat16)
        self.keep_copy(chunk).start()
        for d in range(1, self.far_count):
            self.back_copy(chunk, d).start()

    def run_near_back(self, chunk):
        self.keep_copy(chunk).wait()
        for d in range(1, self.far_count):
            self.back_copy(chunk, d).wait_recv()
        self.near_back(chunk).start()

    def run_last(self, chunk):
        self.near_back(chunk).wait_recv()
        self.last_copy(chunk).start()

    def finish(self, chunk):
        self.last_copy(chunk).wait_recv()
        for d in range(1, self.seq_count):
            self.side_copy(chunk, d).wait_send()
        self.near_copy(chunk).wait_send()
        for d in range(1, self.far_count):
            self.peer_copy(chunk, d).wait_send()
            self.back_copy(chunk, d).wait_send()
        self.near_back(chunk).wait_send()
        self.last_copy(chunk).wait_send()

    def tick(self, number):
        stages = (self.run_near, self.run_peer, self.run_back, self.run_near_back, self.run_last, self.finish)
        for late, stage in enumerate(stages):
            if 0 <= number - late < self.count:
                stage(number - late)


def closing_kernel(
    g1_ref, rows_ref, memt_ref, gain_ref, atta_ref, totala_ref, qa_ref, paira_ref,
    attb_ref, totalb_ref, qb_ref, pairb_ref, dmem_ref, small_ref, qseg_ref, kseg_ref, mseg_ref,
    wqkv_ref, wquery_ref, wkv_ref, wout_ref, early_ref, conv_ref,
    da1_ref, dmemory_ref, out_ref,
    turned_ref, branch_ref, gt_ref, dqa_ref, dqb_ref, dpaira_ref, dpairb_ref, kmark_ref, mmark_ref,
    dkh_ref, dvh_ref, dkm_ref, dvm_ref, dqh_ref, qrow_ref, grow_ref, weight_ref, slope_ref,
    late_ref, kept_ref, core_ref, across_ref, close_ref, piece_ref, mine_ref,
    send_sem, recv_sem, local_sem, kept_sem, conv_sem,
):
    tokens, width = g1_ref.shape
    keys = rows_ref.shape[0]
    place = lax.axis_index("seq")
    seq_count, _, half, early = early_ref.shape
    conv_size = conv_ref.shape[-1]
    share = ShareSum(
        seq_count, half, out_ref.shape[-1], out_ref, core_ref, across_ref, close_ref, piece_ref, mine_ref,
        (send_sem, recv_sem, local_sem),
    )
    step = share.step
    early_count = early // step
    middle_count = (conv_size + 5 * width + step - 1) // step
    share.enter()
    slots = kept_ref.shape[0]

    def kept_copy(chunk):
        return pltpu.make_async_copy(
            early_ref.at[:, share.core, :, share.columns(chunk)], kept_ref.at[chunk % slots], kept_sem.at[chunk]
        )

    conv_copy = pltpu.make_async_copy(conv_ref, late_ref.at[:, :, :, :conv_size], conv_sem)
    for chunk in range(early_count):
        share.core_copy(chunk, early_ref, chunk).start()
    for chunk in range(slots):
        kept_copy(chunk).start()
    conv_copy.start()

    def store_late(start, values):
        size = values.shape[1]
        late_ref[:, :, :, start : start + size] = values.astype(jnp.bfloat16).reshape(seq_count, 2, half, size)

    def start_late(first, count):
        for chunk in range(first, first + count):
            share.core_copy(early_count + chunk, late_ref, chunk).start()

    def side_early(first):
        for chunk in range(first, min(first + slots, early_count)):
            share.core_copy(chunk, early_ref, chunk).wait_recv()
            kept_copy(chunk).wait()
            share.run_side(chunk, kept_ref[chunk % slots])
            if chunk + slots < early_count:
                kept_copy(chunk + slots).start()

    def side_late(first, count):
        for chunk in range(first, first + count):
            share.core_copy(early_count + chunk, late_ref, chunk).wait_recv()
            share.run_side(
                early_count + chunk, late_ref[:, share.core, :, chunk * step : (chunk + 1) * step]
            )

    own = pl.ds(pl.multiple_of(place * tokens, 128), tokens)
    for low, high in row_tiles(keys, 128):
        normed, _ = rows_normed(rows_ref[low:high, :].astype(jnp.float32))
        turned_ref[:, low:high] = (normed * gain_ref[...]).astype(jnp.bfloat16).T
    branch_ref[...] = g1_ref[...].astype(jnp.bfloat16).T
    conv_copy.wait()
    store_late(conv_size, nt_dot(branch_ref[...], atta_ref[...]))
    store_late(conv_size + width, nt_dot(branch_ref[...], attb_ref[...]))
    gt_ref[...] = nn_dot(wout_ref[width:, :], branch_ref[...]).astype(jnp.bfloat16)
    side_early(0)
    attend_back_core(
        H_CROSS, False, 0, qb_ref, pairb_ref, gt_ref, attb_ref, totalb_ref, qseg_ref, mseg_ref,
        dqb_ref, dpairb_ref, mmark_ref, dkm_ref, dvm_ref, dqh_ref, qrow_ref, grow_ref, weight_ref, slope_ref,
    )
    for first in range(slots, early_count, slots):
        side_early(first)
    at = conv_size + 2 * width
    store_late(at, nt_dot(memt_ref[...], dpairb_ref[...]))
    store_late(at + 2 * width, nt_dot(turned_ref[:, own], dqb_ref[...]))
    at = at + 3 * width
    after = middle_count * step
    if at < after:
        late_ref[:, :, :, at:after] = jnp.zeros((seq_count, 2, half, after - at), jnp.bfloat16)
    start_late(0, middle_count)
    dmemory_ref[...] = (dmem_ref[...].astype(jnp.float32) + nn_dot(wkv_ref[...], dpairb_ref[...])).T.astype(jnp.bfloat16)
    gt_ref[...] = nn_dot(wout_ref[:width, :], branch_ref[...]).astype(jnp.bfloat16)

    def pump(k):
        @pl.when(k == 1)
        def _():
            side_late(0, middle_count)

        @pl.when(k >= 1)
        def _():
            share.run_near(k - 1)

        @pl.when(k >= 2)
        def _():
            share.run_peer(k - 2)

        @pl.when(k >= 3)
        def _():
            share.run_back(k - 3)

    attend_back_core(
        H_SELF, True, place, qa_ref, paira_ref, gt_ref, atta_ref, totala_ref, qseg_ref, kseg_ref,
        dqa_ref, dpaira_ref, kmark_ref, dkh_ref, dvh_ref, dqh_ref, qrow_ref, grow_ref, weight_ref, slope_ref, pump,
    )
    ticks = H_SELF // BWD_HEADS - 1
    share.tick(ticks)
    store_late(after, nt_dot(turned_ref[:, own], dqa_ref[...]))
    for low, high in chunks(2 * width):
        store_late(after + width + low, nt_dot(turned_ref[...], dpaira_ref[low:high, :]))
    share.tick(ticks + 1)
    gain_sum = jnp.zeros((8, width), jnp.float32)
    for away in range(seq_count):
        start = lax.rem(place + away, seq_count) * tokens
        for low, high in row_tiles(tokens, 128):
            lanes = pl.ds(pl.multiple_of(start + low, 128), high - low)
            upstream = nn_dot(wqkv_ref[:, width:], dpaira_ref[:, lanes])
            if away == 0:
                upstream = upstream + nn_dot(wqkv_ref[:, :width], dqa_ref[:, low:high])
                upstream = upstream + nn_dot(wquery_ref[...], dqb_ref[:, low:high])
            upstream = upstream.T
            normed, _ = rows_normed(rows_ref[lanes, :].astype(jnp.float32))
            gain_sum = gain_sum + folded(upstream * normed)
            da1_ref[lanes, :] = upstream.astype(jnp.bfloat16)
    small = small_ref[...]
    is_first = lax.broadcasted_iota(jnp.int32, small.shape, 0) == 0
    small = jnp.where(is_first, jnp.sum(gain_sum, axis=0, keepdims=True), small)
    at = after + 3 * width
    store_late(at, small.T)
    at = at + small.shape[0]
    if at < late_ref.shape[-1]:
        late_ref[:, :, :, at:] = jnp.zeros((seq_count, 2, half, late_ref.shape[-1] - at), jnp.bfloat16)
    last_count = share.count - early_count - middle_count
    start_late(middle_count, last_count)
    share.tick(ticks + 2)
    side_late(middle_count, last_count)
    for number in range(ticks + 3, share.count + 5):
        share.tick(number)
    for chunk in range(early_count):
        share.core_copy(chunk, early_ref, chunk).wait_send()
    for chunk in range(share.count - early_count):
        share.core_copy(early_count + chunk, late_ref, chunk).wait_send()


def closing(
    g1, row_inputs, mem_turned, gain, self_kept, cross_kept, d_mem, small, own_seg, seg_row, mem_seg,
    qkv, query, pairs_weight, out, early, conv,
):
    tokens, width = g1.shape
    keys, mems = row_inputs.shape[0], mem_turned.shape[1]
    seq_count = keys // tokens
    half = width // (2 * seq_count)
    far_count = lax.axis_size("rows") // 4
    step = 2 * far_count * LANE_GROUP
    size = width // H_CROSS
    middle_total = conv.shape[1] + 5 * width
    middle_total = middle_total + -middle_total % step
    last_total = 3 * width + small.shape[0]
    last_total = last_total + -last_total % step
    early_total = early.shape[1]
    late = middle_total + last_total
    count = (early_total + late) // step
    slots = 3 + (seq_count - 1) + 2 * far_count
    kept_slots = max(1, 2**19 // (seq_count * half * step))
    low, full = jnp.bfloat16, jnp.float32
    longest = max(tokens, mems)
    v = pltpu.VMEM
    in_hbm = pl.BlockSpec(memory_space=pl.ANY)
    dma = pltpu.SemaphoreType.DMA
    d_normed, d_memory, share = pl.pallas_call(
        closing_kernel,
        out_shape=(
            jax.ShapeDtypeStruct((keys, width), low),
            jax.ShapeDtypeStruct((mems, width), low),
            jax.ShapeDtypeStruct((2, half, early_total + late), low),
        ),
        in_specs=[IN_VMEM] * 21 + [in_hbm] * 2,
        out_specs=(IN_VMEM, IN_VMEM, in_hbm),
        scratch_shapes=[
            v((width, keys), low),
            v((width, tokens), low),
            v((width, tokens), low),
            v((width, tokens), low),
            v((width, tokens), low),
            v((2 * width, keys), low),
            v((2 * width, mems), low),
            v((SEG_ROWS, keys), low),
            v((SEG_ROWS, mems), low),
            v((BWD_HEADS, width // H_SELF, keys), full),
            v((BWD_HEADS, width // H_SELF, keys), full),
            v((BWD_HEADS, size, mems), full),
            v((BWD_HEADS, size, mems), full),
            v((BWD_HEADS, size, tokens), full),
            v((BWD_HEADS, size + SEG_ROWS, tokens), low),
            v((BWD_HEADS, size + SEG_ROWS, tokens), low),
            v((2, longest, TILE), low),
            v((2, longest, TILE), low),
            v((seq_count, 2, half, late), low),
            v((kept_slots, seq_count, half, step), low),
            v((count, seq_count, half, step), low),
            v((count, seq_count - 1, half, step), low),
            v((count, half, step // 2), low),
            v((count, far_count - 1, half, LANE_GROUP), low),
            v((count, half, LANE_GROUP), low),
            dma((count, slots)),
            dma((count, slots)),
            dma((count,)),
            dma((early_total // step,)),
            dma(()),
        ],
        compiler_params=pltpu.CompilerParams(
            collective_id=0, has_side_effects=True, vmem_limit_bytes=HOST_VMEM
        ),
        cost_estimate=pl.CostEstimate(
            flops=tokens * width * width * 200, bytes_accessed=tokens * width * 40, transcendentals=tokens * width * 20
        ),
        name="closing",
    )(
        g1, row_inputs, mem_turned, gain, *self_kept, *cross_kept, d_mem, small,
        own_seg[None], seg_row[None], mem_seg[None], qkv, query, pairs_weight, out,
        early.reshape(seq_count, 2, half, early_total), conv.reshape(seq_count, 2, half, conv.shape[1]),
    )
    return d_normed, d_memory, share.reshape(2 * half, early_total + late), early_total, early_total + middle_total


def segment_reach(seg_row):
    length = seg_row.shape[0]
    first = jnp.sum(seg_row == 0)
    second = first + jnp.sum(seg_row == 1)
    spots = jnp.arange(length, dtype=jnp.int32)
    start = jnp.where(seg_row == 0, 0, jnp.where(seg_row == 1, first, second))
    stop = jnp.where(seg_row == 0, first, jnp.where(seg_row == 1, second, length))
    return spots - start, stop - 1 - spots


def turned_dot(weight, values):
    return jnp.einsum("kn,tk->nt", weight, values, preferred_element_type=jnp.float32)


def out_dot(turned, weight):
    return jnp.einsum("nt,nk->tk", turned, weight, preferred_element_type=jnp.float32)


def weight_dot(values, turned):
    return jnp.einsum("tk,nt->kn", values, turned, preferred_element_type=jnp.float32)


def out_weight_dot(turned, grads_in):
    return jnp.einsum("nt,tk->kn", turned, grads_in, preferred_element_type=jnp.float32)


def turned_back(grads_in, weight):
    return jnp.einsum("tk,nk->nt", grads_in, weight, preferred_element_type=jnp.float32)


def input_back(turned, weight):
    return jnp.einsum("nt,kn->tk", turned, weight, preferred_element_type=jnp.float32)


def self_attend(normed, normed_row, weight, head_count, own_seg, seg_row):
    model_width = normed.shape[1]
    queries = turned_dot(weight[:, :model_width], normed).astype(jnp.bfloat16)
    pairs = turned_dot(weight[:, model_width:], normed_row).astype(jnp.bfloat16)
    att_out, totals = attend_forward(queries, pairs, head_count, True, own_seg, seg_row)
    return (att_out, totals, queries, pairs, normed_row)


def self_back(normed, weight, grad_att, kept, head_count, own_seg, seg_row):
    att_out, totals, queries, pairs, normed_row = kept
    model_width = normed.shape[1]
    d_query, d_pairs = attend_back(
        queries, pairs, grad_att, att_out, totals, head_count, True, own_seg, seg_row
    )
    d_weight = jnp.concatenate([weight_dot(normed, d_query), weight_dot(normed_row, d_pairs)], 1)
    d_normed = input_back(d_query, weight[:, :model_width]) + row_sum_owned(
        input_back(d_pairs, weight[:, model_width:]).astype(jnp.bfloat16)
    )
    return (d_normed, d_weight)


def local(
    hidden_in,
    memory,
    grad_out,
    seg_ids,
    mem_seg_ids,
    gains,
    qkv_first,
    query_cross,
    kv_cross,
    out_first,
    taps_left,
    proj_left,
    taps_right,
    proj_right,
    mid_gain,
    taps_mid,
    proj_mid,
    qkv_second,
    out_second,
    query_last,
    kv_last,
    out_last,
    ffn_up,
    ffn_down,
):
    shards = (
        gains,
        qkv_first,
        query_cross,
        kv_cross,
        out_first,
        taps_left,
        proj_left,
        taps_right,
        proj_right,
        mid_gain,
        taps_mid,
        proj_mid,
        qkv_second,
        out_second,
        query_last,
        kv_last,
        out_last,
        ffn_up,
        ffn_down,
    )
    shard_dims = (1, 0, 0, 0, 1, 1, 0, 1, 0, 0, 1, 1, 0, 0, 0, 0, 0, 0, 1)
    small = (0, 5, 7, 9, 10)
    seq_count = lax.axis_size("seq")

    def select(group):
        return [shards[k] for k in group], [shard_dims[k] for k in group]

    first_group, second_group, conv_group, middle_group = (1,), (2, 3, 4), (6, 8, 11), (12, 13, 14, 15, 16, 17, 18)
    hidden_more = seq_rotated(hidden_in[0])
    first_same = seq_rotated(packed_half(*select(first_group)))
    gains, taps_left, taps_right, mid_gain, taps_mid = small_gather(*select(small))
    first_other = [core_swapped(piece) for piece in first_same]
    (qkv_first,) = joined_group(*select(first_group), interleaved(first_same, first_other), 2)
    packed, _ = after((packed_half(*select(second_group)), memory[0]), first_same)
    second_same, mem_more = seq_rotated(packed[0]), seq_rotated(packed[1])
    row_inputs = in_place_order([hidden_in[0]] + hidden_more, 0)
    mem_rows = in_place_order([memory[0]] + mem_more, 0)
    inputs = hidden_in[0].astype(jnp.float32)
    seg_row = seg_ids[0]
    mem_seg = mem_seg_ids[0]
    tok_count, model_width = inputs.shape
    row_start = lax.axis_index("seq") * tok_count
    own_seg = lax.dynamic_slice_in_dim(seg_row, row_start, tok_count)
    since, left = segment_reach(seg_row)
    since = lax.dynamic_slice_in_dim(jnp.pad(since, (RIM, 0)), row_start, tok_count + RIM)[:, None]
    left = lax.dynamic_slice_in_dim(jnp.pad(left, (0, RIM)), row_start, tok_count + RIM)[:, None]
    gain_rows = gains.astype(jnp.float32)
    mid_gain_f = mid_gain.astype(jnp.float32)
    left_taps = taps_left.astype(jnp.float32)
    right_taps = taps_right.astype(jnp.float32)
    mid_taps = taps_mid.astype(jnp.float32)
    normed_a = layer_norm(inputs, gain_rows[0]).astype(jnp.bfloat16)
    normed_row = layer_norm(row_inputs.astype(jnp.float32), gain_rows[0]).astype(jnp.bfloat16)
    normed_a, second_same = after(normed_a, second_same)
    second_other = [core_swapped(piece) for piece in second_same]
    packed, _ = after((packed_quarter(*select(conv_group)), packed_quarter(*select(middle_group))), second_same)
    conv_same, middle_same = seq_rotated(packed[0]), seq_rotated(packed[1])
    kept_a = self_attend(normed_a, normed_row, qkv_first, H_SELF, own_seg, seg_row)
    att_a, (second_other, conv_same) = after(kept_a[0], (second_other, conv_same))
    kept_a = (att_a,) + kept_a[1:]
    conv_near = [near_swapped(piece) for piece in conv_same]
    query_cross, kv_cross, out_first = joined_group(*select(second_group), interleaved(second_same, second_other), 2)
    pairs_b = turned_dot(kv_cross, mem_rows).astype(jnp.bfloat16)
    query_b = turned_dot(query_cross, normed_a).astype(jnp.bfloat16)
    out_b, total_b = attend_forward(query_b, pairs_b, H_CROSS, False, own_seg, mem_seg)
    out_b, conv_near = after(out_b, conv_near)
    conv_across = [core_swapped(jnp.concatenate(pair, 0)) for pair in zip(conv_same, conv_near)]
    hidden_b = (
        inputs
        + out_dot(kept_a[0], out_first[:model_width])
        + out_dot(out_b, out_first[model_width:])
    )
    hidden_b, middle_same = after(hidden_b, middle_same)
    middle_near = [near_swapped(piece) for piece in middle_same]
    proj_left, proj_right, proj_mid = joined_group(
        *select(conv_group), interleaved(conv_same, conv_near, conv_across), 4
    )
    normed_c = layer_norm(hidden_b, gain_rows[1]).astype(jnp.bfloat16)
    conv_l, conv_r, conv_m, hidden_c, normed_d = conv_forward(
        hidden_b,
        normed_c,
        passed_along(normed_c[tok_count - RIM :], "seq", 1),
        since,
        left_taps,
        right_taps,
        mid_taps,
        mid_gain_f[None],
        gain_rows[2:3],
        proj_left,
        proj_right,
        proj_mid,
    )
    normed_d, middle_near = after(normed_d, middle_near)
    middle_across = [core_swapped(jnp.concatenate(pair, 0)) for pair in zip(middle_same, middle_near)]
    middle_pieces = interleaved(middle_same, middle_near, middle_across)
    down_at = sum(shard.shape[1] for shard in shards[12:18])
    down, _ = joined_weight(shards[18], 1, middle_pieces, down_at, 4)
    conv_rims = passed_along(jnp.concatenate([conv_l[:RIM], conv_r[:RIM]], 1), "seq", -1)
    more = jnp.stack(seq_rotated(normed_d))
    result, grad_now, d_normed, d_middle, d_gains_late, d_mem = middle(
        hidden_c,
        normed_d,
        more,
        mem_rows,
        grad_out[0],
        gain_rows[3:5],
        own_seg,
        seg_row,
        mem_seg,
        down,
        shards[12:18],
        middle_pieces,
    )
    d_hidden, g_three = norm_back(hidden_c, gain_rows[2], row_sum_owned(d_normed))
    grad_now = grad_now + d_hidden
    branch = grad_now.astype(jnp.bfloat16)
    grad_now, d_projections, d_taps_left, d_taps_right, d_taps_mid, d_mid_gain, g_two = conv_back(
        grad_now,
        passed_along(branch[:RIM], "seq", -1),
        conv_l,
        conv_r,
        conv_rims,
        conv_m,
        normed_c,
        hidden_b,
        left,
        left_taps,
        right_taps,
        mid_taps,
        mid_gain_f[None],
        gain_rows[1:2],
        proj_left,
        proj_right,
        proj_mid,
    )
    d_mid_gain, g_two = d_mid_gain[0], g_two[0]
    d_gains = jnp.concatenate([jnp.stack([jnp.zeros_like(g_two), g_two, g_three], 0), d_gains_late], 0)
    wide, narrow = proj_left.shape[1], proj_right.shape[1]
    width = model_width // lax.axis_size("seq")
    small_grads = (d_gains, d_taps_left, d_taps_right, d_mid_gain, d_taps_mid)
    d_normed, d_memory, share, second_at, third_at = closing(
        grad_now,
        row_inputs,
        mem_rows.T,
        gain_rows[:1],
        kept_a[:4],
        (out_b, total_b, query_b, pairs_b),
        d_mem,
        small_rows(small_grads, width),
        own_seg,
        seg_row,
        mem_seg,
        qkv_first,
        query_cross,
        kv_cross,
        out_first,
        d_middle,
        d_projections,
    )
    d_hidden, _ = norm_back(inputs, gain_rows[0], row_sum_owned(d_normed))
    grad_in = grad_now + d_hidden
    grad_mem = row_sum_owned(d_memory)
    shares = [None] * len(shards)
    up = down.shape[0]
    for offset, group, sizes in (
        (
            0,
            (17, 18, 16, 14, 15, 12, 13),
            (up, up, model_width, model_width, 2 * model_width, 3 * model_width, model_width),
        ),
        (
            second_at,
            (11, 6, 8, 4, 3, 2),
            (wide, wide, narrow, 2 * model_width, 2 * model_width, model_width),
        ),
        (third_at, (1,), (3 * model_width,)),
    ):
        for k, size in zip(group, sizes):
            piece = share[:, offset : offset + size].astype(jnp.float32)
            shares[k] = piece if shard_dims[k] == 0 else piece.T
            offset = offset + size
    parts = small_shares(share[:, offset : offset + 128].astype(jnp.float32), small_grads, width)
    for k, piece in zip(small, parts):
        shares[k] = piece
    return (
        result[None],
        grad_in[None],
        grad_mem[None],
        shares[0],
        shares[1],
        shares[2],
        shares[3],
        shares[4],
        shares[5],
        shares[6],
        shares[7],
        shares[8],
        shares[9],
        shares[10],
        shares[11],
        shares[12],
        shares[13],
        shares[14],
        shares[15],
        shares[16],
        shares[17],
        shares[18],
    )


def solution(mesh):
    placed = (
        P("rows", "seq", None),
        P("rows", "seq", None),
        P("rows", "seq", None),
        P("rows", None),
        P("rows", None),
        P(None, "seq"),
        P("seq", None),
        P("seq", None),
        P("seq", None),
        P(None, "seq"),
        P(None, "seq"),
        P("seq", None),
        P(None, "seq"),
        P("seq", None),
        P("seq"),
        P(None, "seq"),
        P(None, "seq"),
        P("seq", None),
        P("seq", None),
        P("seq", None),
        P("seq", None),
        P("seq", None),
        P("seq", None),
        P(None, "seq"),
    )
    return jax.shard_map(
        local,
        mesh=mesh,
        in_specs=placed,
        out_specs=(
            P("rows", "seq", None),
            P("rows", "seq", None),
            P("rows", "seq", None),
            P(None, "seq"),
            P("seq", None),
            P("seq", None),
            P("seq", None),
            P(None, "seq"),
            P(None, "seq"),
            P("seq", None),
            P(None, "seq"),
            P("seq", None),
            P("seq"),
            P(None, "seq"),
            P(None, "seq"),
            P("seq", None),
            P("seq", None),
            P("seq", None),
            P("seq", None),
            P("seq", None),
            P("seq", None),
            P(None, "seq"),
        ),
        check_vma=False,
    )
```

profile of v0, /device:TPU:0, one launch (start us, length us, event | category | flops | bytes accessed | tf_op | source)
XLA Modules:
  0.0 446.9 jit_solution(17148020794969195187)
XLA Ops:
  5.6 3.0 collective-permute-start.2
  10.4 2.0 collective-permute-start.4
  30.8 1.8 pad_maximum_fusion.1
  36.0 2.0 collective-permute-start.3
  38.1 4.4 collective-permute-done.7
  43.5 1.9 convert_reduce_fusion
  48.1 2.1 convolution_convert_fusion.refs_1_.paira_ref
  50.3 4.1 collective-permute-done.3
  57.5 9.1 %attend_fwd.2 = (bf16[512,640]{1,0:T(8,128)(2,1)S(1)}, f32[16,1,640]{2,1,0:T(1,128)S(1)}) custom-call(s32[1]{0:T(128)} %bitcast.place_ref, bf16[512,640]{1,0:T(8,128)(2,1)S(1)} %convolution_convert_fusion.2.refs_0_.qa_ref, bf16[1024,1280]{1,0:T(8,128)(2,1)S(1)} %convolution_convert_fusion.refs_1_.paira_ref, ...), custom_call_target="tpu_custom_call" | custom-call | flops 7864320000 | bytes 2621440 | tf_op jit(solution)/shard_map/attend_fwd/pallas_call | solution.py:513
  71.4 3.4 attend_fwd.3
  78.5 8.9 %collective-permute-done.9.rest_0_ = bf16[64,8192]{1,0:T(8,128)(2,1)} collective-permute-done((bf16[64,8192]{1,0:T(8,128)(2,1)S(1)}, bf16[64,8192]{1,0:T(8,128)(2,1)}, u32[]{:S(2)}, u32[]{:S(2)}) %collective-permute-start.9) | collective-permute-done | bytes 1048608 | tf_op jit(solution)/shard_map/ppermute | solution.py:24
  88.1 3.4 collective-permute-start.10
  97.9 16.9 %conv_fwd.1 = (bf16[640,512]{1,0:T(8,128)(2,1)S(1)}, bf16[640,512]{1,0:T(8,128)(2,1)S(1)}, bf16[640,1024]{1,0:T(8,128)(2,1)}, f32[640,512]{1,0:T(8,128)}, bf16[640,512]{1,0:T(8,128)(2,1)S(1)}) custom-call(f32[640,512]{1,0:T(8,128)} %copy-done.21, bf16[640,512]{1,0:T(8,128)(2,1)S(1)} %multiply_convert_fusion.a2_ref, ...), custom_call_target="tpu_custom_call" | custom-call | flops 6710886400 | bytes 5242880 | tf_op jit(solution)/shard_map/conv_fwd/pallas_call | solution.py:692
  114.9 2.3 collective-permute-done.12.rest_1_
  117.1 3.2 pad_maximum_fusion
  128.9 2.0 maximum_select_fusion.down_ref
  130.9 12.4 %collective-permute-done.13 = bf16[640,512]{1,0:T(8,128)(2,1)S(1)} collective-permute-done((bf16[640,512]{1,0:T(8,128)(2,1)S(1)}, bf16[640,512]{1,0:T(8,128)(2,1)S(1)}, u32[]{:S(2)}, u32[]{:S(2)}) %collective-permute-start.13) | collective-permute-done | bytes 655392 | tf_op jit(solution)/shard_map/ppermute | solution.py:24
  144.1 56.5 %middle.1 = (bf16[640,512]{1,0:T(8,128)(2,1)}, f32[640,512]{1,0:T(8,128)}, bf16[1280,512]{1,0:T(8,128)(2,1)}, bf16[512,8192]{1,0:T(8,128)(2,1)}, f32[2,512]{1,0:T(2,128)}, /*index=5*/bf16[512,256]{1,0:T(8,128)(2,1)}) custom-call(s32[3]{0:T(128)} %pad_add_fusion.place_ref, f32[640,512]{1,0:T(8,128)} %get-tuple-element.76.h2_ref, bf16[640,512]{1,0:T(8,128)(2,1)} %copy-done.10, ...), custom_call_target="tpu_custom_call" | custom-call | flops 33554432000 | bytes 13107200 | tf_op jit(solution)/shard_map/middle/pallas_call | solution.py:1062
  200.6 2.0 constant_dynamic-slice_fusion.2
  202.6 12.4 %collective-permute-start.15 = (bf16[640,512]{1,0:T(8,128)(2,1)}, bf16[640,512]{1,0:T(8,128)(2,1)}, u32[]{:S(2)}, u32[]{:S(2)}) collective-permute-start(bf16[640,512]{1,0:T(8,128)(2,1)} %constant_dynamic-slice_fusion.2), channel_id=1, source_target_pairs={{0,1},{1,0},{2,3},{3,2},{4,5},{5,4},{6,7},{7,6},{8,9},{9,8},{10,11... | collective-permute-start | bytes 1966088 | tf_op jit(solution)/shard_map/ppermute | solution.py:176
  219.6 10.9 %collective-permute-done.15 = bf16[640,512]{1,0:T(8,128)(2,1)} collective-permute-done((bf16[640,512]{1,0:T(8,128)(2,1)}, bf16[640,512]{1,0:T(8,128)(2,1)}, u32[]{:S(2)}, u32[]{:S(2)}) %collective-permute-start.15) | collective-permute-done | bytes 655392 | tf_op jit(solution)/shard_map/ppermute | solution.py:176
  230.4 2.1 fusion.25
  234.4 4.3 collective-permute-done.16.brim_ref
  238.7 27.6 %conv_bwd.1 = (f32[640,512]{1,0:T(8,128)S(1)}, bf16[512,2304]{1,0:T(8,128)(2,1)}, f32[11,512]{1,0:T(8,128)S(1)}, f32[7,512]{1,0:T(8,128)S(1)}, f32[7,1024]{1,0:T...) custom-call(f32[640,512]{1,0:T(8,128)} %copy-done.29, bf16[16,512]{1,0:T(8,128)(2,1)S(1)} %collective-permute-done.16.brim_ref, ...), custom_call_target="tpu_custom_call" | custom-call | flops 13421772800 | bytes 13107200 | tf_op jit(solution)/shard_map/conv_bwd/pallas_call | solution.py:850
  269.8 130.9 %closing.1 = (bf16[1280,512]{1,0:T(8,128)(2,1)}, bf16[256,512]{1,0:T(8,128)(2,1)}, bf16[2,128,15360]{2,1,0:T(8,128)(2,1)}) custom-call(f32[640,512]{1,0:T(8,128)} %copy-done, bf16[1280,512]{1,0:T(8,128)(2,1)} %copy-done.23, bf16[512,256]{1,0:T(8,128)(2,1)} %bitcast.169, f32[1,512]{1,0:T(1,128)} %copy-done.52, bf16[512,640]{1,0:T(8,128)(2,1)} %copy-done.2, ...), custom_call_target="tpu_custom_call" | custom-call | flops 33554432000 | bytes 13107200 | tf_op jit(solution)/shard_map/closing/pallas_call | solution.py:1455
  401.6 3.4 slice_convert_fusion.1
  405.1 3.7 slice_convert_fusion.3
  411.1 3.3 fusion.43
  415.3 7.7 %collective-permute-start.18 = (bf16[640,512]{1,0:T(8,128)(2,1)}, bf16[640,512]{1,0:T(8,128)(2,1)}, u32[]{:S(2)}, u32[]{:S(2)}) collective-permute-start(bf16[640,512]{1,0:T(8,128)(2,1)} %constant_dynamic-slice_fusion.1), channel_id=1, source_target_pairs={{0,1},{1,0},{2,3},{3,2},{4,5},{5,4},{6,7},{7,6},{8,9},{9,8},{10,11... | collective-permute-start | bytes 1966088 | tf_op jit(solution)/shard_map/ppermute | solution.py:176
  434.5 2.8 slice_convert_fusion.6
  438.9 2.5 collective-permute-done.19
  443.1 1.9 fusion.27
  (323 shorter events, 88.4 us)
Async XLA Ops:
  0.7 11.7 %copy-start.19 = (bf16[1,640,512]{2,1,0:T(8,128)(2,1)S(1)}, bf16[1,640,512]{2,1,0:T(8,128)(2,1)}, u32[]{:S(2)}) copy-start(bf16[1,640,512]{2,1,0:T(8,128)(2,1)} %param.24) | copy-start | bytes 1966084
  0.7 12.3 %copy-start.34 = (bf16[1024,256]{1,0:T(8,128)(2,1)S(1)}, bf16[1024,256]{1,0:T(8,128)(2,1)}, u32[]{:S(2)}) copy-start(bf16[1024,256]{1,0:T(8,128)(2,1)} %param.33) | copy-start | bytes 1572868
  5.6 29.0 %collective-permute-start.2 = (bf16[80,128]{1,0:T(8,128)(2,1)S(1)}, bf16[80,128]{1,0:T(8,128)(2,1)S(1)}, u32[]{:S(2)}, u32[]{:S(2)}) collective-permute-start(bf16[80,128]{1,0:T(8,128)(2,1)S(1)} %pad_bitcast_fusion), channel_id=1, source_target_pairs={{1,0},{0,1},{3,2},{2,3},{5,4},{4,5},{7,6},{6,7},{9,8},{8,9},{11,10... | collective-permute-start | bytes 61448 | tf_op jit(solution)/shard_map/ppermute | solution.py:24
  10.3 25.6 %collective-permute-start = (bf16[128,1536]{1,0:T(8,128)(2,1)}, bf16[128,1536]{1,0:T(8,128)(2,1)}, u32[]{:S(2)}, u32[]{:S(2)}) collective-permute-start(bf16[128,1536]{1,0:T(8,128)(2,1)} %constant_dynamic-slice_fusion.11), channel_id=1, source_target_pairs={{1,0},{0,1},{3,2},{2,3},{5,4},{4,5},{7,6},{6,7},{9,8},{8,9},{11,10... | collective-permute-start | bytes 1179656 | tf_op jit(solution)/shard_map/ppermute | solution.py:24
  10.4 33.1 %collective-permute-start.4 = (bf16[640,512]{1,0:T(8,128)(2,1)}, bf16[640,512]{1,0:T(8,128)(2,1)}, u32[]{:S(2)}, u32[]{:S(2)}) collective-permute-start(bf16[640,512]{1,0:T(8,128)(2,1)} %bitcast.154), channel_id=1, source_target_pairs={{1,0},{0,1},{3,2},{2,3},{5,4},{4,5},{7,6},{6,7},{9,8},{8,9},{11,10... | collective-permute-start | bytes 1966088 | tf_op jit(solution)/shard_map/ppermute | solution.py:24
  33.3 37.9 %copy-start.5 = (s32[1,640]{1,0:T(1,128)}, s32[1,640]{1,0:T(1,128)S(1)}, u32[]{:S(2)}) copy-start(s32[1,640]{1,0:T(1,128)S(1)} %constant_dynamic-slice_fusion.7.refs_2_.qseg_ref) | copy-start | bytes 7684
  34.6 13.5 %copy-start.52 = (f32[1,512]{1,0:T(1,128)}, f32[1,512]{1,0:T(1,128)S(1)}, u32[]{:S(2)}) copy-start(f32[1,512]{1,0:T(1,128)S(1)} %get-tuple-element.192.gain_ref) | copy-start | bytes 6148
  35.9 6.5 %collective-permute-start.7 = (bf16[128,512]{0,1:T(8,128)(2,1)S(1)}, bf16[128,512]{0,1:T(8,128)(2,1)}, u32[]{:S(2)}, u32[]{:S(2)}) collective-permute-start(bf16[128,512]{0,1:T(8,128)(2,1)S(1)} %bitcast.181), channel_id=1, source_target_pairs={{1,0},{0,1},{3,2},{2,3},{5,4},{4,5},{7,6},{6,7},{9,8},{8,9},{11,10... | collective-permute-start | bytes 393224 | tf_op jit(solution)/shard_map/ppermute | solution.py:24
  36.0 18.3 %collective-permute-start.3 = (bf16[128,2560]{1,0:T(8,128)(2,1)}, bf16[128,2560]{1,0:T(8,128)(2,1)S(1)}, u32[]{:S(2)}, u32[]{:S(2)}) collective-permute-start(bf16[128,2560]{1,0:T(8,128)(2,1)} %pad_maximum_fusion.1), channel_id=1, source_target_pairs={{1,0},{0,1},{3,2},{2,3},{5,4},{4,5},{7,6},{6,7},{9,8},{8,9},{11,10... | collective-permute-start | bytes 1966088 | tf_op jit(solution)/shard_map/ppermute | solution.py:24
  38.1 8.1 %collective-permute-start.1 = (bf16[128,1536]{1,0:T(8,128)(2,1)}, bf16[128,1536]{1,0:T(8,128)(2,1)S(1)}, u32[]{:S(2)}, u32[]{:S(2)}) collective-permute-start(bf16[128,1536]{1,0:T(8,128)(2,1)} %collective-permute-done), channel_id=1, source_target_pairs={{0,2},{2,0},{4,6},{6,4},{8,10},{10,8},{12,14},{14,12},{16,18},{18,... | collective-permute-start | bytes 1179656 | tf_op jit(solution)/shard_map/ppermute | solution.py:28
  43.5 27.2 %copy-start.37 = (bf16[256,512]{0,1:T(8,128)(2,1)}, bf16[256,512]{0,1:T(8,128)(2,1)S(1)}, u32[]{:S(2)}) copy-start(bf16[256,512]{0,1:T(8,128)(2,1)S(1)} %maximum_select_fusion.17) | copy-start | bytes 786436
  54.3 12.3 %collective-permute-start.5 = (bf16[128,2560]{1,0:T(8,128)(2,1)S(1)}, bf16[128,2560]{1,0:T(8,128)(2,1)S(1)}, u32[]{:S(2)}, u32[]{:S(2)}) collective-permute-start(bf16[128,2560]{1,0:T(8,128)(2,1)S(1)} %collective-permute-done.3), channel_id=1, source_target_pairs={{0,2},{2,0},{4,6},{6,4},{8,10},{10,8},{12,14},{14,12},{16,18},{18,... | collective-permute-start | bytes 1966088 | tf_op jit(solution)/shard_map/ppermute | solution.py:28
  55.3 11.2 %copy-start.14 = (bf16[512,640]{1,0:T(8,128)(2,1)}, bf16[512,640]{1,0:T(8,128)(2,1)S(1)}, u32[]{:S(2)}) copy-start(bf16[512,640]{1,0:T(8,128)(2,1)S(1)} %convolution_convert_fusion.2.refs_0_.qa_ref) | copy-start | bytes 1966084
  55.3 11.3 %collective-permute-start.6 = (bf16[64,2304]{1,0:T(8,128)(2,1)S(1)}, bf16[64,2304]{1,0:T(8,128)(2,1)S(1)}, u32[]{:S(2)}, u32[]{:S(2)}) collective-permute-start(bf16[64,2304]{1,0:T(8,128)(2,1)S(1)} %copy-done.47), channel_id=1, source_target_pairs={{1,0},{0,1},{3,2},{2,3},{5,4},{4,5},{7,6},{6,7},{9,8},{8,9},{11,10... | collective-permute-start | bytes 884744 | tf_op jit(solution)/shard_map/ppermute | solution.py:24
  56.0 31.4 %collective-permute-start.9 = (bf16[64,8192]{1,0:T(8,128)(2,1)S(1)}, bf16[64,8192]{1,0:T(8,128)(2,1)}, u32[]{:S(2)}, u32[]{:S(2)}) collective-permute-start(bf16[64,8192]{1,0:T(8,128)(2,1)S(1)} %copy-done.51), channel_id=1, source_target_pairs={{1,0},{0,1},{3,2},{2,3},{5,4},{4,5},{7,6},{6,7},{9,8},{8,9},{11,10... | collective-permute-start | bytes 3145736 | tf_op jit(solution)/shard_map/ppermute | solution.py:24
  66.6 11.3 %copy-start.2 = (bf16[512,640]{1,0:T(8,128)(2,1)}, bf16[512,640]{1,0:T(8,128)(2,1)S(1)}, u32[]{:S(2)}) copy-start(bf16[512,640]{1,0:T(8,128)(2,1)S(1)} %get-tuple-element.67.atta_ref) | copy-start | bytes 1966084
  66.7 8.9 %collective-permute-start.8 = (bf16[64,2304]{1,0:T(8,128)(2,1)S(1)}, bf16[64,2304]{1,0:T(8,128)(2,1)S(1)}, u32[]{:S(2)}, u32[]{:S(2)}) collective-permute-start(bf16[64,2304]{1,0:T(8,128)(2,1)S(1)} %collective-permute-done.6), channel_id=1, source_target_pairs={{0,4},{2,6},{4,0},{6,2},{8,12},{10,14},{12,8},{14,10},{16,20},{18,... | collective-permute-start | bytes 884744 | tf_op jit(solution)/shard_map/ppermute | solution.py:50
  76.7 16.5 %collective-permute-start.11 = (bf16[128,2304]{1,0:T(8,128)(2,1)}, bf16[128,2304]{1,0:T(8,128)(2,1)}, u32[]{:S(2)}, u32[]{:S(2)}) collective-permute-start(bf16[128,2304]{1,0:T(8,128)(2,1)} %pad_maximum_fusion.2), channel_id=1, source_target_pairs={{0,2},{2,0},{4,6},{6,4},{8,10},{10,8},{12,14},{14,12},{16,18},{18,... | collective-permute-start | bytes 1769480 | tf_op jit(solution)/shard_map/ppermute | solution.py:28
  78.5 9.4 %copy-start.21 = (f32[640,512]{1,0:T(8,128)}, f32[640,512]{1,0:T(8,128)S(1)}, u32[]{:S(2)}) copy-start(f32[640,512]{1,0:T(8,128)S(1)} %fusion.13.h1_ref) | copy-start | bytes 3932164
  88.1 9.8 %collective-permute-start.10 = (bf16[16,512]{1,0:T(8,128)(2,1)S(1)}, bf16[16,512]{1,0:T(8,128)(2,1)S(1)}, u32[]{:S(2)}, u32[]{:S(2)}) collective-permute-start(bf16[16,512]{1,0:T(8,128)(2,1)S(1)} %slice.293), channel_id=1, source_target_pairs={{0,1},{2,3},{4,5},{6,7},{8,9},{10,11},{12,13},{14,15},{16,17},{18,... | collective-permute-start | bytes 49160 | tf_op jit(solution)/shard_map/ppermute | solution.py:195
  91.5 25.6 %collective-permute-start.12 = (bf16[64,8192]{1,0:T(8,128)(2,1)}, bf16[64,8192]{1,0:T(8,128)(2,1)S(1)}, u32[]{:S(2)}, u32[]{:S(2)}) collective-permute-start(bf16[64,8192]{1,0:T(8,128)(2,1)} %collective-permute-done.9.rest_0_), channel_id=1, source_target_pairs={{0,4},{2,6},{4,0},{6,2},{8,12},{10,14},{12,8},{14,10},{16,20},{18,... | collective-permute-start | bytes 3145736 | tf_op jit(solution)/shard_map/ppermute | solution.py:50
  120.3 5.9 %collective-permute-start.14 = (bf16[128,8192]{1,0:T(8,128)(2,1)}, bf16[128,8192]{1,0:T(8,128)(2,1)}, u32[]{:S(2)}, u32[]{:S(2)}) collective-permute-start(bf16[128,8192]{1,0:T(8,128)(2,1)} %pad_maximum_fusion), channel_id=1, source_target_pairs={{0,2},{2,0},{4,6},{6,4},{8,10},{10,8},{12,14},{14,12},{16,18},{18,... | collective-permute-start | bytes 6291464 | tf_op jit(solution)/shard_map/ppermute | solution.py:28
  126.2 17.1 %collective-permute-start.13 = (bf16[640,512]{1,0:T(8,128)(2,1)S(1)}, bf16[640,512]{1,0:T(8,128)(2,1)S(1)}, u32[]{:S(2)}, u32[]{:S(2)}) collective-permute-start(bf16[640,512]{1,0:T(8,128)(2,1)S(1)} %copy-done.11), channel_id=1, source_target_pairs={{1,0},{0,1},{3,2},{2,3},{5,4},{4,5},{7,6},{6,7},{9,8},{8,9},{11,10... | collective-permute-start | bytes 1966088 | tf_op jit(solution)/shard_map/ppermute | solution.py:24
  202.6 27.8 %collective-permute-start.15 = (bf16[640,512]{1,0:T(8,128)(2,1)}, bf16[640,512]{1,0:T(8,128)(2,1)}, u32[]{:S(2)}, u32[]{:S(2)}) collective-permute-start(bf16[640,512]{1,0:T(8,128)(2,1)} %constant_dynamic-slice_fusion.2), channel_id=1, source_target_pairs={{0,1},{1,0},{2,3},{3,2},{4,5},{5,4},{6,7},{7,6},{8,9},{9,8},{10,11... | collective-permute-start | bytes 1966088 | tf_op jit(solution)/shard_map/ppermute | solution.py:176
  216.5 13.9 %copy-start.22 = (f32[640,512]{1,0:T(8,128)S(1)}, f32[640,512]{1,0:T(8,128)}, u32[]{:S(2)}) copy-start(f32[640,512]{1,0:T(8,128)} %get-tuple-element.76.h2_ref) | copy-start | bytes 3932164
  216.5 17.9 %collective-permute-start.17 = (bf16[16,1024]{1,0:T(8,128)(2,1)S(1)}, bf16[16,1024]{1,0:T(8,128)(2,1)S(1)}, u32[]{:S(2)}, u32[]{:S(2)}) collective-permute-start(bf16[16,1024]{1,0:T(8,128)(2,1)S(1)} %pad_maximum_fusion.4), channel_id=1, source_target_pairs={{1,0},{3,2},{5,4},{7,6},{9,8},{11,10},{13,12},{15,14},{17,16},{19,... | collective-permute-start | bytes 98312 | tf_op jit(solution)/shard_map/ppermute | solution.py:195
  233.1 5.6 %collective-permute-start.16 = (bf16[16,512]{1,0:T(8,128)(2,1)S(1)}, bf16[16,512]{1,0:T(8,128)(2,1)S(1)}, u32[]{:S(2)}, u32[]{:S(2)}) collective-permute-start(bf16[16,512]{1,0:T(8,128)(2,1)S(1)} %slice.355), channel_id=1, source_target_pairs={{1,0},{3,2},{5,4},{7,6},{9,8},{11,10},{13,12},{15,14},{17,16},{19,... | collective-permute-start | bytes 49160 | tf_op jit(solution)/shard_map/ppermute | solution.py:195
  238.7 30.0 %copy-start.58 = (f32[2,512]{1,0:T(2,128)S(1)}, f32[2,512]{1,0:T(2,128)}, u32[]{:S(2)}) copy-start(f32[2,512]{1,0:T(2,128)} %get-tuple-element.92) | copy-start | bytes 12292
  414.4 8.6 %copy-start.48 = (bf16[256,512]{1,0:T(8,128)(2,1)S(1)}, bf16[256,512]{1,0:T(8,128)(2,1)}, u32[]{:S(2)}) copy-start(bf16[256,512]{1,0:T(8,128)(2,1)} %get-tuple-element.100) | copy-start | bytes 786436
  415.3 27.7 %collective-permute-start.18 = (bf16[640,512]{1,0:T(8,128)(2,1)}, bf16[640,512]{1,0:T(8,128)(2,1)}, u32[]{:S(2)}, u32[]{:S(2)}) collective-permute-start(bf16[640,512]{1,0:T(8,128)(2,1)} %constant_dynamic-slice_fusion.1), channel_id=1, source_target_pairs={{0,1},{1,0},{2,3},{3,2},{4,5},{5,4},{6,7},{7,6},{8,9},{9,8},{10,11... | collective-permute-start | bytes 1966088 | tf_op jit(solution)/shard_map/ppermute | solution.py:176
  423.7 17.7 %collective-permute-start.19 = (bf16[128,512]{1,0:T(8,128)(2,1)}, bf16[128,512]{1,0:T(8,128)(2,1)}, u32[]{:S(2)}, u32[]{:S(2)}) collective-permute-start(bf16[128,512]{1,0:T(8,128)(2,1)} %constant_dynamic-slice_fusion), channel_id=1, source_target_pairs={{0,1},{1,0},{2,3},{3,2},{4,5},{5,4},{6,7},{7,6},{8,9},{9,8},{10,11... | collective-permute-start | bytes 393224 | tf_op jit(solution)/shard_map/ppermute | solution.py:176
  434.5 8.6 %copy-start.53 = (f32[1,512]{1,0:T(1,128)S(1)}, f32[1,512]{1,0:T(1,128)}, u32[]{:S(2)}) copy-start(f32[1,512]{1,0:T(1,128)} %copy-done.52) | copy-start | bytes 6148
  (51 other events, 188.3 us)
where the time goes:
time: 455 us; the launch traced here: 447 us
  Pallas kernels  244 us (54%)
  local copies, waits for them, and re-layouts  54.4 us (12%)
  other arithmetic  50.8 us (11%)
  waiting for transfers between devices  49.9 us (11%)
  starting transfers between devices  38.8 us (9%)
  matrix products  4.89 us (1%)
    pallas_call x1, Pallas kernels, closing(): pl.pallas_call(closing_kernel, out_shape=(jax.ShapeDtypeStruct((keys, wid...  131 us
    pallas_call x1, Pallas kernels, middle(): pl.pallas_call(functools.partial(middle_kernel, len(pieces)), out_shape=(...  56.5 us
    ppermute x8, waiting for transfers between devices, rotated(): lax.ppermute(block, axis, [((i + distance) % size, i) for i in range(size)])  29.7 us
    pallas_call x1, Pallas kernels, conv_back(): pl.pallas_call(conv_bwd_kernel, out_shape=(jax.ShapeDtypeStruct((tokens,...  27.6 us
    unnamed x145, local copies, waits for them, and re-layouts  24.7 us
    ppermute x3, starting transfers between devices, halved_sum(): lax.ppermute(sent, axis, [(i, i ^ bit) for i in range(lax.axis_size(axis))])  20.2 us
    pallas_call x1, Pallas kernels, conv_forward(): pl.pallas_call(conv_fwd_kernel, out_shape=(jax.ShapeDtypeStruct((tokens,...  16.9 us
    ppermute x3, waiting for transfers between devices, halved_sum(): lax.ppermute(sent, axis, [(i, i ^ bit) for i in range(lax.axis_size(axis))])  13.4 us
  transfers between devices with their start and end apart: 20, of which 9 were waited for; matrix products, arithmetic and copies ran while one was open for 17% of the time, Pallas kernels for 7%

commit v1 on v0

--- a/solution.py
+++ b/solution.py
@@ -153,19 +153,6 @@
         for grad in grads
     ]
     return padded_rows(jnp.concatenate(rows, 0), 128, 0)
-
-
-def small_shares(columns, grads, width):
-    seq_count = lax.axis_size("seq")
-    rows = columns.T
-    results = []
-    offset = 0
-    for grad in grads:
-        count = grad.size // (seq_count * width)
-        shape = grad.shape[:-1] + (grad.shape[-1] // seq_count,)
-        results.append(rows[offset : offset + count].reshape(shape))
-        offset = offset + count
-    return results
 
 
 def halved_sum(block, axis, bit, dim):
@@ -501,9 +488,11 @@
 IN_SMEM = pl.BlockSpec(memory_space=pltpu.SMEM)
 IN_VMEM = pl.BlockSpec(memory_space=pltpu.VMEM)
 KERNEL_VMEM = 48 * 2**20
+HOST_VMEM = 63 * 2**20 + 2**19
 
 
 LANE_GROUP = 128
+SWAP_TICK = 4
 
 
 def attend_forward(queries, pairs_t, heads, causal, query_seg, key_seg):
@@ -735,13 +724,31 @@
 
 def conv_bwd_kernel(
     g2_ref, brim_ref, cl_ref, clrim_ref, cr_ref, crrim_ref, cm_ref, a2_ref, h1_ref, left_ref,
-    tl_ref, tr_ref, tm_ref, mgain_ref, gain_ref, pl_ref, pr_ref, pm_ref,
-    g1_ref, dw_ref, dtl_ref, dtr_ref, dtm_ref, dmgain_ref, dgain_ref,
+    tl_ref, tr_ref, tm_ref, mgain_ref, gain_ref, pl_ref, pr_ref, pm_ref, across_in_ref, second_ref,
+    g1_ref, dw_ref, dtl_ref, dtr_ref, dtm_ref, dmgain_ref, dgain_ref, mine_ref, across_out_ref,
     bext_ref, cle_ref, cre_ref, wide_ref, grad_ref, up_ref, back_ref, normed_ref, inv_ref, dpl_ref, dpr_ref, a2f_ref,
+    kept_ref, core_ref, across_ref, close_ref, piece_ref, send_sem, recv_sem, kept_sem,
 ):
     tokens, width = g2_ref.shape
     total = tokens + RIM
     wide, narrow = pl_ref.shape[1], pr_ref.shape[1]
+    share = ShareSum(
+        send_sem, recv_sem, core=core_ref, across=across_ref, close=close_ref, piece=piece_ref, mine=mine_ref
+    )
+    first_count = mine_ref.shape[0]
+    step = share.step
+    firsts, seconds = range(first_count), range(first_count, first_count + core_ref.shape[0])
+    share.core_first = first_count
+    share.enter([share.mate, share.close] + share.peers[1:] + share.sides[1:])
+    kept_copy = pltpu.make_async_copy(
+        second_ref.at[:, share.core, :, : kept_ref.shape[-1]], kept_ref, kept_sem
+    )
+    kept_copy.start()
+    for chunk in seconds:
+        share.core_copy(chunk, second_ref, chunk - first_count).start()
+    for chunk in firsts:
+        share.early_sums[chunk] = across_in_ref.at[:, chunk * step : (chunk + 1) * step]
+        share.near_copy(chunk).start()
     bext_ref[:tokens, :] = g2_ref[...].astype(jnp.bfloat16)
     bext_ref[tokens:, :] = brim_ref[...]
     cle_ref[:tokens, :] = cl_ref[...]
@@ -756,6 +763,12 @@
         grad_ref[low:high, :] = nt_dot(bext_ref[low:high, :], pm_ref[...])
         up_ref[low:high, :] = nn_dot(cle_ref[low:high, :], pl_ref[...])
         back_ref[low:high, :narrow] = nn_dot(cre_ref[low:high, :], pr_ref[...])
+
+    kept_copy.wait()
+    for chunk in seconds:
+        at = (chunk - first_count) * step
+        share.core_copy(chunk, second_ref, chunk - first_count).wait_recv()
+        share.run_side(chunk, kept_ref[:, :, at : at + step])
 
     def merge_rows(rows):
         pre = up_ref[rows, :]
@@ -794,6 +807,8 @@
         dpr_ref[rows, :] = d_merged[:, :narrow].astype(jnp.bfloat16)
 
     loop_rows(total, MERGE_ROWS, merge_back)
+    for chunk in firsts:
+        share.run_peer(chunk)
     gain_sum = jnp.zeros((8, wide), jnp.float32)
 
     def gain_rows(k, held):
@@ -838,15 +853,33 @@
 
     gain_sum = lax.fori_loop(0, tokens // 64, finish, jnp.zeros((8, width), jnp.float32))
     dgain_ref[...] = jnp.sum(gain_sum, axis=0, keepdims=True)
+    for chunk in firsts:
+        share.peer_sum(chunk)
+        share.near_copy(chunk).wait_send()
+        share.sent_peers(chunk)
+    for chunk in seconds:
+        at = (chunk - first_count) * step
+        across_out_ref[:, at : at + step] = share.side_sum(chunk, first_count)
+        share.core_copy(chunk, second_ref, chunk - first_count).wait_send()
+        share.sent_sides(chunk)
 
 
 def conv_back(
-    g2, brim, c_l, c_r, rims, c_m, a2, h1, left, taps_l, taps_r, taps_m, mid_gain, gain, proj_left, proj_right, proj_mid
+    g2, brim, c_l, c_r, rims, c_m, a2, h1, left, taps_l, taps_r, taps_m, mid_gain, gain, proj_left, proj_right, proj_mid,
+    across, second,
 ):
     tokens, width = g2.shape
     wide, narrow = proj_left.shape[1], proj_right.shape[1]
     total = tokens + RIM
     low, full = jnp.bfloat16, jnp.float32
+    seq_count, far_count = lax.axis_size("seq"), lax.axis_size("rows") // 4
+    half = width // (2 * seq_count)
+    step = 2 * far_count * LANE_GROUP
+    first_count, second_count = across.shape[1] // step, second.shape[1] // step - 1
+    count = first_count + second_count
+    slots = 1 + seq_count + far_count
+    in_hbm = pl.BlockSpec(memory_space=pl.ANY)
+    dma = pltpu.SemaphoreType.DMA
     return pl.pallas_call(
         conv_bwd_kernel,
         out_shape=(
@@ -857,9 +890,11 @@
             jax.ShapeDtypeStruct(taps_m.shape, full),
             jax.ShapeDtypeStruct((1, wide), full),
             jax.ShapeDtypeStruct((1, width), full),
+            jax.ShapeDtypeStruct((first_count, half, LANE_GROUP), low),
+            jax.ShapeDtypeStruct((half, second_count * step), low),
         ),
-        in_specs=[IN_VMEM] * 18,
-        out_specs=(IN_VMEM,) * 7,
+        in_specs=[IN_VMEM] * 19 + [in_hbm],
+        out_specs=(IN_VMEM,) * 9,
         scratch_shapes=[
             pltpu.VMEM((total, width), low),
             pltpu.VMEM((total, width), low),
@@ -873,8 +908,18 @@
             pltpu.VMEM((total, wide), low),
             pltpu.VMEM((total, narrow), low),
             pltpu.VMEM((tokens, width), full),
+            pltpu.VMEM((seq_count, half, second_count * step), low),
+            pltpu.VMEM((second_count, seq_count, half, step), low),
+            pltpu.VMEM((second_count, seq_count - 1, half, step), low),
+            pltpu.VMEM((first_count, half, step // 2), low),
+            pltpu.VMEM((first_count, far_count - 1, half, LANE_GROUP), low),
+            dma((count, slots)),
+            dma((count, slots)),
+            dma(()),
         ],
-        compiler_params=pltpu.CompilerParams(vmem_limit_bytes=KERNEL_VMEM),
+        compiler_params=pltpu.CompilerParams(
+            collective_id=1, has_side_effects=True, vmem_limit_bytes=HOST_VMEM
+        ),
         cost_estimate=pl.CostEstimate(
             flops=tokens * width * wide * 40, bytes_accessed=tokens * width * 40, transcendentals=tokens * wide
         ),
@@ -882,6 +927,7 @@
     )(
         g2, brim, c_l, rims[:, :width], c_r, rims[:, width:], c_m, a2, h1, left,
         taps_l, taps_r, taps_m, mid_gain, gain, proj_left, proj_right, proj_mid,
+        across, second.reshape(seq_count, 2, half, second.shape[1]),
     )
 
 
@@ -953,20 +999,23 @@
 
 def middle_kernel(
     piece_count,
-    place_ref, h2_ref, a3_ref, a3more_ref, mem_ref, gout_ref, gain_ref, qseg_ref, kseg_ref, mseg_ref, down_ref,
+    h2_ref, a3_ref, a3more_ref, mem_ref, gout_ref, gain_ref, qseg_ref, kseg_ref, mseg_ref, down_ref,
     qkv_own, out2_own, query_own, kv_own, out_own, up_own, *rest,
 ):
     pieces, rest = rest[:piece_count], rest[piece_count:]
     (
-        result_ref, g3_ref, da3_ref, dw_ref, dgain_ref, dmem_ref,
+        result_ref, g3_ref, da3_ref, dw_ref, dgain_ref, dmem_ref, across_out_ref,
         wqkv_ref, wout2_ref, wquery_ref, wkv_ref, wout_ref, wup_ref, sems,
         turned_ref, memt_ref, a4_ref, a4t_ref, qt_ref, pair_ref, attc_ref, totalc_ref,
         qdt_ref, paird_ref, attd_ref, totald_ref, h3_ref, h4_ref, act_ref, dup_ref, low_ref, gt_ref, dq_ref, dpair_ref, dpaird_ref,
         back_ref, wide_ref, kmark_ref, mmark_ref, sum_ref, peak_ref, score_ref,
         dkh_ref, dvh_ref, dkm_ref, dvm_ref, dqh_ref, qrow_ref, grow_ref, weight_ref, slope_ref,
+        first_ref, core_ref, across_ref, send_sem, recv_sem,
     ) = rest
     tokens, width = h2_ref.shape
-    place, near, core = place_ref[0], place_ref[1], place_ref[2]
+    share = ShareSum(send_sem, recv_sem, core=core_ref, across=across_ref)
+    place, near, core = share.place, share.near, share.core
+    share.enter([share.mate] + share.sides[1:])
     seq_count = piece_count // 3 + 1
     high_width = wup_ref.shape[1]
     first, copies = [], []
@@ -1011,11 +1060,20 @@
     for low, high in chunks(tokens):
         result_ref[low:high, :] = (h4_ref[low:high, :] + nn_dot(act_ref[low:high, :], down_ref[...])).astype(jnp.bfloat16)
         back_ref[low:high, :] = nt_dot(dup_ref[low:high, :], wup_ref[...])
+    seq_count, _, half, first_total = first_ref.shape
+    firsts = range(first_total // share.step)
+
+    def store_first(start, values):
+        size = values.shape[1]
+        first_ref[:, :, :, start : start + size] = values.astype(jnp.bfloat16).reshape(seq_count, 2, half, size)
+
     for left, right in row_tiles(high_width, 512):
-        store_grad(dw_ref, left, tn_dot(a4_ref[...], dup_ref[:, left:right]))
-        store_grad(dw_ref, high_width + left, tn_dot(gout_ref[...], act_ref[:, left:right]))
-
-    at = 2 * high_width
+        store_first(left, tn_dot(a4_ref[...], dup_ref[:, left:right]))
+        store_first(high_width + left, tn_dot(gout_ref[...], act_ref[:, left:right]))
+
+    for chunk in firsts:
+        share.core_copy(chunk, first_ref, chunk).start()
+    at = 0
     dgain_ref[1:2, :] = norm_back_into(h4_ref, gout_ref, h4_ref, gain_ref[1:2, :], back_ref)
     low_ref[...] = h4_ref[...].astype(jnp.bfloat16)
     store_grad(dw_ref, at, nn_dot(attd_ref[...], low_ref[...]))
@@ -1026,6 +1084,9 @@
     )
     store_grad(dw_ref, at + width, nt_dot(a4t_ref[...], dq_ref[...]))
     store_grad(dw_ref, at + 2 * width, nt_dot(memt_ref[...], dpaird_ref[...]))
+    for chunk in firsts:
+        share.core_copy(chunk, first_ref, chunk).wait_recv()
+        share.run_side(chunk, first_ref[:, core, :, chunk * share.step : (chunk + 1) * share.step])
     dmem_ref[...] = nn_dot(wkv_ref[...], dpaird_ref[...]).astype(jnp.bfloat16)
     back_ref[...] = nn_dot(wquery_ref[...], dq_ref[...]).T
     dgain_ref[0:1, :] = norm_back_into(g3_ref, h4_ref, h3_ref, gain_ref[0:1, :], back_ref)
@@ -1045,6 +1106,10 @@
         wide_ref[low:high, own] += nn_dot(wqkv_ref[low:high, :width], dq_ref[...])
     for low, high in row_tiles(wide_ref.shape[1], tokens):
         da3_ref[low:high, :] = wide_ref[:, low:high].T.astype(jnp.bfloat16)
+    for chunk in firsts:
+        across_out_ref[:, chunk * share.step : (chunk + 1) * share.step] = share.side_sum(chunk)
+        share.core_copy(chunk, first_ref, chunk).wait_send()
+        share.sent_sides(chunk)
 
 
 def middle(h2, a3, a3_more, mem_rows, grad_out, gains, own_seg, seg_row, mem_seg, down, owns, pieces):
@@ -1057,20 +1122,23 @@
     longest = max(tokens, mems)
     v = pltpu.VMEM
     in_hbm = pl.BlockSpec(memory_space=pl.ANY)
-    row = lax.axis_index("rows")
-    places = jnp.stack([lax.axis_index("seq"), (row // 2) % 2, row % 2]).astype(jnp.int32)
+    half = width // (2 * seq_count)
+    step = lax.axis_size("rows") // 2 * LANE_GROUP
+    count = 2 * high_width // step
+    dma = pltpu.SemaphoreType.DMA
     return pl.pallas_call(
         functools.partial(middle_kernel, len(pieces)),
         out_shape=(
             jax.ShapeDtypeStruct((tokens, width), low),
             jax.ShapeDtypeStruct((tokens, width), full),
             jax.ShapeDtypeStruct((keys, width), low),
-            jax.ShapeDtypeStruct((width, 2 * high_width + 8 * width), low),
+            jax.ShapeDtypeStruct((width, 8 * width), low),
             jax.ShapeDtypeStruct((2, width), full),
             jax.ShapeDtypeStruct((width, mems), low),
+            jax.ShapeDtypeStruct((half, 2 * high_width), low),
         ),
-        in_specs=[IN_SMEM] + [IN_VMEM] * 10 + [in_hbm] * (6 + len(pieces)),
-        out_specs=(IN_VMEM,) * 6,
+        in_specs=[IN_VMEM] * 10 + [in_hbm] * (6 + len(pieces)),
+        out_specs=(IN_VMEM,) * 7,
         scratch_shapes=[
             v((width, 3 * width), low),
             v((width, width), low),
@@ -1116,27 +1184,31 @@
             v((BWD_HEADS, size + SEG_ROWS, tokens), low),
             v((2, longest, TILE), low),
             v((2, longest, TILE), low),
+            v((seq_count, 2, half, 2 * high_width), low),
+            v((count, seq_count, half, step), low),
+            v((count, seq_count - 1, half, step), low),
+            dma((count, seq_count)),
+            dma((count, seq_count)),
         ],
-        compiler_params=pltpu.CompilerParams(vmem_limit_bytes=MIDDLE_VMEM),
+        compiler_params=pltpu.CompilerParams(
+            collective_id=0, has_side_effects=True, vmem_limit_bytes=HOST_VMEM
+        ),
         cost_estimate=pl.CostEstimate(
             flops=tokens * width * width * 200, bytes_accessed=tokens * width * 40, transcendentals=tokens * width * 20
         ),
         name="middle",
     )(
-        places, h2, a3, a3_more, mem_rows, grad_out, gains, own_seg[None], seg_row[None], mem_seg[None], down,
+        h2, a3, a3_more, mem_rows, grad_out, gains, own_seg[None], seg_row[None], mem_seg[None], down,
         *owns, *pieces,
     )
 
 
-HOST_VMEM = 63 * 2**20 + 2**19
-
-
 class ShareSum:
-    def __init__(self, seq_count, half, total, out_ref, core_ref, across_ref, close_ref, piece_ref, mine_ref, sems):
-        self.seq_count, self.half, self.total = seq_count, half, total
-        self.out_ref, self.core_ref, self.across_ref = out_ref, core_ref, across_ref
-        self.close_ref, self.piece_ref, self.mine_ref = close_ref, piece_ref, mine_ref
-        self.send_sem, self.recv_sem, self.local_sem = sems
+    def __init__(self, send_sem, recv_sem, core=None, across=None, close=None, piece=None, mine=None, out=None, local_sem=None):
+        self.send_sem, self.recv_sem, self.local_sem = send_sem, recv_sem, local_sem
+        self.core_ref, self.across_ref, self.close_ref = core, across, close
+        self.piece_ref, self.mine_ref, self.out_ref = piece, mine, out
+        self.seq_count = lax.axis_size("seq")
         self.far_count = lax.axis_size("rows") // 4
         row, place = lax.axis_index("rows"), lax.axis_index("seq")
         self.core, self.near, self.far, self.place = lax.rem(row, 2), lax.rem(row // 2, 2), row // 4, place
@@ -1146,14 +1218,14 @@
             (lax.rem(self.far + d, self.far_count) * 4 + self.near * 2 + self.core, place)
             for d in range(1, self.far_count)
         ]
-        self.sides = [None] + [(row, lax.rem(place + d, seq_count)) for d in range(1, seq_count)]
+        self.sides = [None] + [(row, lax.rem(place + d, self.seq_count)) for d in range(1, self.seq_count)]
         self.step = 2 * self.far_count * LANE_GROUP
         self.wide = self.far_count * LANE_GROUP
-        self.count = total // self.step
-
-    def enter(self):
+        self.core_first = 0
+        self.early_sums = {}
+
+    def enter(self, friends):
         barrier = pltpu.get_barrier_semaphore()
-        friends = [self.mate, self.close] + self.peers[1:] + self.sides[1:]
         for friend in friends:
             pl.semaphore_signal(barrier, inc=1, device_id=friend, device_id_type=pl.DeviceIdType.MESH)
         pl.semaphore_wait(barrier, len(friends))
@@ -1172,16 +1244,21 @@
         )
 
     def core_copy(self, chunk, source_ref, at):
-        return self.copy(chunk, 0, source_ref.at[:, 1 - self.core, :, self.columns(at)], self.core_ref.at[chunk], self.mate)
+        return self.copy(chunk, 0, source_ref.at[:, 1 - self.core, :, self.columns(at)], self.core_ref.at[chunk - self.core_first], self.mate)
 
     def side_copy(self, chunk, d):
         away = lax.rem(self.place + d, self.seq_count)
-        return self.copy(chunk, d, self.core_ref.at[chunk, away], self.across_ref.at[chunk, d - 1], self.sides[d])
+        return self.copy(chunk, d, self.core_ref.at[chunk - self.core_first, away], self.across_ref.at[chunk - self.core_first, d - 1], self.sides[d])
+
+    def sum_at(self, chunk):
+        if chunk in self.early_sums:
+            return self.early_sums[chunk]
+        return self.across_ref.at[chunk - self.core_first, 0]
 
     def near_copy(self, chunk):
         lanes = pl.ds(pl.multiple_of((1 - self.near) * self.wide, LANE_GROUP), self.wide)
         return self.copy(
-            chunk, self.seq_count, self.across_ref.at[chunk, 0, :, lanes], self.close_ref.at[chunk], self.close
+            chunk, self.seq_count, self.sum_at(chunk).at[:, lanes], self.close_ref.at[chunk], self.close
         )
 
     def peer_copy(self, chunk, d):
@@ -1219,28 +1296,32 @@
         return self.copy(chunk, self.seq_count + 2 * self.far_count, block, block, self.mate)
 
     def run_side(self, chunk, kept):
-        self.core_ref[chunk] = (kept.astype(jnp.float32) + self.core_ref[chunk].astype(jnp.float32)).astype(jnp.bfloat16)
+        at = chunk - self.core_first
+        self.core_ref[at] = (kept.astype(jnp.float32) + self.core_ref[at].astype(jnp.float32)).astype(jnp.bfloat16)
         for d in range(1, self.seq_count):
             self.side_copy(chunk, d).start()
 
-    def run_near(self, chunk):
+    def side_sum(self, chunk, first=0):
         for d in range(1, self.seq_count):
             self.side_copy(chunk, d).wait_recv()
-        summed = self.core_ref[chunk, self.place].astype(jnp.float32)
+        summed = self.core_ref[chunk - first, self.place].astype(jnp.float32)
         for d in range(1, self.seq_count):
-            summed = summed + self.across_ref[chunk, d - 1].astype(jnp.float32)
-        self.across_ref[chunk, 0] = summed.astype(jnp.bfloat16)
+            summed = summed + self.across_ref[chunk - first, d - 1].astype(jnp.float32)
+        return summed.astype(jnp.bfloat16)
+
+    def run_near(self, chunk):
+        self.sum_at(chunk)[...] = self.side_sum(chunk, self.core_first)
         self.near_copy(chunk).start()
 
     def run_peer(self, chunk):
         self.near_copy(chunk).wait_recv()
         lanes = pl.ds(pl.multiple_of(self.near * self.wide, LANE_GROUP), self.wide)
-        summed = self.across_ref[chunk, 0, :, lanes].astype(jnp.float32) + self.close_ref[chunk].astype(jnp.float32)
+        summed = self.sum_at(chunk)[:, lanes].astype(jnp.float32) + self.close_ref[chunk].astype(jnp.float32)
         self.close_ref[chunk] = summed.astype(jnp.bfloat16)
         for d in range(1, self.far_count):
             self.peer_copy(chunk, d).start()
 
-    def run_back(self, chunk):
+    def peer_sum(self, chunk):
         for d in range(1, self.far_count):
             self.peer_copy(chunk, d).wait_recv()
         lanes = pl.ds(pl.multiple_of(self.far * LANE_GROUP, LANE_GROUP), LANE_GROUP)
@@ -1248,6 +1329,12 @@
         for d in range(1, self.far_count):
             summed = summed + self.piece_ref[chunk, d - 1].astype(jnp.float32)
         self.mine_ref[chunk] = summed.astype(jnp.bfloat16)
+
+    def run_back(self, chunk):
+        self.peer_sum(chunk)
+        self.start_back(chunk)
+
+    def start_back(self, chunk):
         self.keep_copy(chunk).start()
         for d in range(1, self.far_count):
             self.back_copy(chunk, d).start()
@@ -1262,140 +1349,167 @@
         self.near_back(chunk).wait_recv()
         self.last_copy(chunk).start()
 
-    def finish(self, chunk):
-        self.last_copy(chunk).wait_recv()
+    def sent_sides(self, chunk):
         for d in range(1, self.seq_count):
             self.side_copy(chunk, d).wait_send()
-        self.near_copy(chunk).wait_send()
+
+    def sent_peers(self, chunk):
         for d in range(1, self.far_count):
             self.peer_copy(chunk, d).wait_send()
+
+    def sent_backs(self, chunk):
+        for d in range(1, self.far_count):
             self.back_copy(chunk, d).wait_send()
         self.near_back(chunk).wait_send()
         self.last_copy(chunk).wait_send()
 
-    def tick(self, number):
-        stages = (self.run_near, self.run_peer, self.run_back, self.run_near_back, self.run_last, self.finish)
-        for late, stage in enumerate(stages):
-            if 0 <= number - late < self.count:
-                stage(number - late)
-
 
 def closing_kernel(
     g1_ref, rows_ref, memt_ref, gain_ref, atta_ref, totala_ref, qa_ref, paira_ref,
     attb_ref, totalb_ref, qb_ref, pairb_ref, dmem_ref, small_ref, qseg_ref, kseg_ref, mseg_ref,
-    wqkv_ref, wquery_ref, wkv_ref, wout_ref, early_ref, conv_ref,
-    da1_ref, dmemory_ref, out_ref,
+    wqkv_ref, wquery_ref, wkv_ref, wout_ref, mine_in_ref, across_in_ref, second_ref, conv_ref,
+    grad_in_ref, grad_mem_ref, out_ref,
     turned_ref, branch_ref, gt_ref, dqa_ref, dqb_ref, dpaira_ref, dpairb_ref, kmark_ref, mmark_ref,
     dkh_ref, dvh_ref, dkm_ref, dvm_ref, dqh_ref, qrow_ref, grow_ref, weight_ref, slope_ref,
-    late_ref, kept_ref, core_ref, across_ref, close_ref, piece_ref, mine_ref,
-    send_sem, recv_sem, local_sem, kept_sem, conv_sem,
+    late_ref, core_ref, across_ref, close_ref, piece_ref, mine_ref,
+    send_sem, recv_sem, local_sem, conv_sem,
+    da1_ref, da1_in_ref, upstream_ref, dmemory_ref, dmemory_in_ref, swap_send, swap_recv,
 ):
     tokens, width = g1_ref.shape
     keys = rows_ref.shape[0]
     place = lax.axis_index("seq")
-    seq_count, _, half, early = early_ref.shape
-    conv_size = conv_ref.shape[-1]
+    seq_count, _, half, conv_size = conv_ref.shape
     share = ShareSum(
-        seq_count, half, out_ref.shape[-1], out_ref, core_ref, across_ref, close_ref, piece_ref, mine_ref,
-        (send_sem, recv_sem, local_sem),
+        send_sem, recv_sem, core=core_ref, across=across_ref, close=close_ref, piece=piece_ref, mine=mine_ref,
+        out=out_ref, local_sem=local_sem,
     )
     step = share.step
-    early_count = early // step
-    middle_count = (conv_size + 5 * width + step - 1) // step
-    share.enter()
-    slots = kept_ref.shape[0]
-
-    def kept_copy(chunk):
-        return pltpu.make_async_copy(
-            early_ref.at[:, share.core, :, share.columns(chunk)], kept_ref.at[chunk % slots], kept_sem.at[chunk]
-        )
-
-    conv_copy = pltpu.make_async_copy(conv_ref, late_ref.at[:, :, :, :conv_size], conv_sem)
-    for chunk in range(early_count):
-        share.core_copy(chunk, early_ref, chunk).start()
-    for chunk in range(slots):
-        kept_copy(chunk).start()
-    conv_copy.start()
+    first_count, second_count = mine_in_ref.shape[0], across_in_ref.shape[1] // step
+    early_count = first_count + second_count
+    count = out_ref.shape[-1] // step
+    extra = second_ref.shape[-1] - second_count * step
+    conv_end = extra + conv_size
+    middle_count = (conv_end + 5 * width + step - 1) // step
+    last_count = count - early_count - middle_count
+    share.core_first = early_count
+    share.enter([share.mate, share.close] + share.peers[1:] + share.sides[1:])
+    late_copies = (
+        pltpu.make_async_copy(second_ref.at[:, :, :, second_count * step :], late_ref.at[:, :, :, :extra], conv_sem.at[0]),
+        pltpu.make_async_copy(conv_ref, late_ref.at[:, :, :, extra:conv_end], conv_sem.at[1]),
+    )
+    for copy in late_copies:
+        copy.start()
+    firsts = range(first_count)
+    seconds = range(first_count, early_count)
+    middles = range(early_count, early_count + middle_count)
+    lasts = range(early_count + middle_count, count)
+    for chunk in firsts:
+        mine_ref[chunk] = mine_in_ref[chunk]
+        share.start_back(chunk)
+    for chunk in seconds:
+        at = (chunk - first_count) * step
+        share.early_sums[chunk] = across_in_ref.at[:, at : at + step]
+        share.near_copy(chunk).start()
 
     def store_late(start, values):
         size = values.shape[1]
         late_ref[:, :, :, start : start + size] = values.astype(jnp.bfloat16).reshape(seq_count, 2, half, size)
 
-    def start_late(first, count):
-        for chunk in range(first, first + count):
-            share.core_copy(early_count + chunk, late_ref, chunk).start()
-
-    def side_early(first):
-        for chunk in range(first, min(first + slots, early_count)):
-            share.core_copy(chunk, early_ref, chunk).wait_recv()
-            kept_copy(chunk).wait()
-            share.run_side(chunk, kept_ref[chunk % slots])
-            if chunk + slots < early_count:
-                kept_copy(chunk + slots).start()
-
-    def side_late(first, count):
-        for chunk in range(first, first + count):
-            share.core_copy(early_count + chunk, late_ref, chunk).wait_recv()
-            share.run_side(
-                early_count + chunk, late_ref[:, share.core, :, chunk * step : (chunk + 1) * step]
-            )
+    def start_late(chunk):
+        share.core_copy(chunk, late_ref, chunk - early_count).start()
+
+    def side_late(chunk):
+        at = (chunk - early_count) * step
+        share.core_copy(chunk, late_ref, chunk - early_count).wait_recv()
+        share.run_side(chunk, late_ref[:, share.core, :, at : at + step])
 
     own = pl.ds(pl.multiple_of(place * tokens, 128), tokens)
+    ready = conv_end // step
+    with_out = (conv_end + 2 * width) // step
+    branch_ref[...] = g1_ref[...].astype(jnp.bfloat16).T
+    for copy in late_copies:
+        copy.wait()
+    for chunk in middles[:ready]:
+        start_late(chunk)
+    store_late(conv_end, nt_dot(branch_ref[...], atta_ref[...]))
+    store_late(conv_end + width, nt_dot(branch_ref[...], attb_ref[...]))
+    for chunk in middles[ready:with_out]:
+        start_late(chunk)
+    for chunk in middles[:ready]:
+        side_late(chunk)
+    gt_ref[...] = nn_dot(wout_ref[width:, :], branch_ref[...]).astype(jnp.bfloat16)
     for low, high in row_tiles(keys, 128):
         normed, _ = rows_normed(rows_ref[low:high, :].astype(jnp.float32))
         turned_ref[:, low:high] = (normed * gain_ref[...]).astype(jnp.bfloat16).T
-    branch_ref[...] = g1_ref[...].astype(jnp.bfloat16).T
-    conv_copy.wait()
-    store_late(conv_size, nt_dot(branch_ref[...], atta_ref[...]))
-    store_late(conv_size + width, nt_dot(branch_ref[...], attb_ref[...]))
-    gt_ref[...] = nn_dot(wout_ref[width:, :], branch_ref[...]).astype(jnp.bfloat16)
-    side_early(0)
+    for chunk in middles[ready:with_out]:
+        side_late(chunk)
     attend_back_core(
         H_CROSS, False, 0, qb_ref, pairb_ref, gt_ref, attb_ref, totalb_ref, qseg_ref, mseg_ref,
         dqb_ref, dpairb_ref, mmark_ref, dkm_ref, dvm_ref, dqh_ref, qrow_ref, grow_ref, weight_ref, slope_ref,
     )
-    for first in range(slots, early_count, slots):
-        side_early(first)
-    at = conv_size + 2 * width
+    at = conv_end + 2 * width
     store_late(at, nt_dot(memt_ref[...], dpairb_ref[...]))
     store_late(at + 2 * width, nt_dot(turned_ref[:, own], dqb_ref[...]))
     at = at + 3 * width
     after = middle_count * step
     if at < after:
         late_ref[:, :, :, at:after] = jnp.zeros((seq_count, 2, half, after - at), jnp.bfloat16)
-    start_late(0, middle_count)
+    for chunk in middles[with_out:]:
+        start_late(chunk)
     dmemory_ref[...] = (dmem_ref[...].astype(jnp.float32) + nn_dot(wkv_ref[...], dpairb_ref[...])).T.astype(jnp.bfloat16)
     gt_ref[...] = nn_dot(wout_ref[:width, :], branch_ref[...]).astype(jnp.bfloat16)
 
+    done = {}
+
+    def advance(chunk):
+        stages = (share.run_near, share.run_peer, share.run_back, share.run_near_back, share.run_last)
+        stages[done.setdefault(chunk, 3 if chunk in firsts else 1 if chunk in seconds else 0)](chunk)
+        done[chunk] += 1
+
+    def advance_all(*groups):
+        for group in groups:
+            for chunk in group:
+                advance(chunk)
+
+    def first_pump():
+        advance_all(seconds, middles[:1])
+
+    def second_pump():
+        for chunk in middles[with_out:]:
+            side_late(chunk)
+        advance_all(firsts, middles[:2])
+
+    def third_pump():
+        advance_all(seconds, middles[:3])
+
+    def fourth_pump():
+        advance_all(firsts, middles[:4])
+
     def pump(k):
-        @pl.when(k == 1)
-        def _():
-            side_late(0, middle_count)
-
-        @pl.when(k >= 1)
-        def _():
-            share.run_near(k - 1)
-
-        @pl.when(k >= 2)
-        def _():
-            share.run_peer(k - 2)
-
-        @pl.when(k >= 3)
-        def _():
-            share.run_back(k - 3)
+        for at, action in enumerate((first_pump, second_pump, third_pump, fourth_pump)):
+            pl.when(k == at)(action)
 
     attend_back_core(
         H_SELF, True, place, qa_ref, paira_ref, gt_ref, atta_ref, totala_ref, qseg_ref, kseg_ref,
         dqa_ref, dpaira_ref, kmark_ref, dkh_ref, dvh_ref, dqh_ref, qrow_ref, grow_ref, weight_ref, slope_ref, pump,
     )
-    ticks = H_SELF // BWD_HEADS - 1
-    share.tick(ticks)
+    entered = [len(middles[:4])]
+    flow = list(middles) + list(lasts)
+
+    def tick():
+        older = [chunk for chunk in flow[: entered[0]] if done[chunk] < 5]
+        advance_all(older, flow[entered[0] : entered[0] + 1])
+        entered[0] += 1
+
+    advance_all(seconds)
+    tick()
     store_late(after, nt_dot(turned_ref[:, own], dqa_ref[...]))
     for low, high in chunks(2 * width):
         store_late(after + width + low, nt_dot(turned_ref[...], dpaira_ref[low:high, :]))
-    share.tick(ticks + 1)
+    start_late(lasts[0])
+    tick()
     gain_sum = jnp.zeros((8, width), jnp.float32)
-    for away in range(seq_count):
+    for away in [*range(1, seq_count), 0]:
         start = lax.rem(place + away, seq_count) * tokens
         for low, high in row_tiles(tokens, 128):
             lanes = pl.ds(pl.multiple_of(start + low, 128), high - low)
@@ -1406,7 +1520,59 @@
             upstream = upstream.T
             normed, _ = rows_normed(rows_ref[lanes, :].astype(jnp.float32))
             gain_sum = gain_sum + folded(upstream * normed)
-            da1_ref[lanes, :] = upstream.astype(jnp.bfloat16)
+            if away == 0:
+                upstream_ref[low:high, :] = upstream
+            else:
+                da1_ref[away - 1, low:high, :] = upstream.astype(jnp.bfloat16)
+
+    def swap(kind, away, source, target):
+        return pltpu.make_async_remote_copy(
+            src_ref=source,
+            dst_ref=target,
+            send_sem=swap_send.at[kind, away - 1],
+            recv_sem=swap_recv.at[kind, away - 1],
+            device_id=share.sides[away],
+            device_id_type=pl.DeviceIdType.MESH,
+        )
+
+    mem_own = dmemory_in_ref.shape[1]
+
+    def row_swap(away):
+        return swap(0, away, da1_ref.at[away - 1], da1_in_ref.at[away - 1])
+
+    def mem_swap(away):
+        start = pl.multiple_of(lax.rem(place + away, seq_count) * mem_own, mem_own)
+        return swap(1, away, dmemory_ref.at[pl.ds(start, mem_own), :], dmemory_in_ref.at[away - 1])
+
+    def start_swaps():
+        for away in range(1, seq_count):
+            pl.when(place + away >= seq_count)(row_swap(away).start)
+            mem_swap(away).start()
+
+    def finish_swaps():
+        for away in range(1, seq_count):
+
+            @pl.when(place < away)
+            def _():
+                row_swap(away).wait_recv()
+                upstream_ref[...] += da1_in_ref[away - 1].astype(jnp.float32)
+
+        own_start = pl.multiple_of(place * tokens, 128)
+        for low, high in row_tiles(tokens, 128):
+            values = rows_ref[pl.ds(pl.multiple_of(own_start + low, 128), high - low), :].astype(jnp.float32)
+            normed, inverse = rows_normed(values)
+            grad_in_ref[low:high, :] = g1_ref[low:high, :] + rows_norm_back(
+                normed, inverse, gain_ref[...], upstream_ref[low:high, :]
+            )
+        total = dmemory_ref[pl.ds(pl.multiple_of(place * mem_own, mem_own), mem_own), :].astype(jnp.float32)
+        for away in range(1, seq_count):
+            mem_swap(away).wait_recv()
+            total = total + dmemory_in_ref[away - 1].astype(jnp.float32)
+        grad_mem_ref[...] = total
+        for away in range(1, seq_count):
+            pl.when(place + away >= seq_count)(row_swap(away).wait_send)
+            mem_swap(away).wait_send()
+
     small = small_ref[...]
     is_first = lax.broadcasted_iota(jnp.int32, small.shape, 0) == 0
     small = jnp.where(is_first, jnp.sum(gain_sum, axis=0, keepdims=True), small)
@@ -1415,21 +1581,33 @@
     at = at + small.shape[0]
     if at < late_ref.shape[-1]:
         late_ref[:, :, :, at:] = jnp.zeros((seq_count, 2, half, late_ref.shape[-1] - at), jnp.bfloat16)
-    last_count = share.count - early_count - middle_count
-    start_late(middle_count, last_count)
-    share.tick(ticks + 2)
-    side_late(middle_count, last_count)
-    for number in range(ticks + 3, share.count + 5):
-        share.tick(number)
-    for chunk in range(early_count):
-        share.core_copy(chunk, early_ref, chunk).wait_send()
-    for chunk in range(share.count - early_count):
-        share.core_copy(early_count + chunk, late_ref, chunk).wait_send()
+    for chunk in lasts[1:]:
+        start_late(chunk)
+    side_late(lasts[0])
+    advance_all(seconds)
+    for chunk in lasts[1:]:
+        side_late(chunk)
+    start_swaps()
+    ticks = 0
+    while any(done.get(chunk, 0) < 5 for chunk in flow):
+        tick()
+        ticks += 1
+        if ticks == SWAP_TICK:
+            finish_swaps()
+    for chunk in range(count):
+        share.last_copy(chunk).wait_recv()
+        share.sent_backs(chunk)
+    for chunk in range(first_count, count):
+        share.near_copy(chunk).wait_send()
+        share.sent_peers(chunk)
+    for chunk in range(early_count, count):
+        share.core_copy(chunk, late_ref, chunk - early_count).wait_send()
+        share.sent_sides(chunk)
 
 
 def closing(
     g1, row_inputs, mem_turned, gain, self_kept, cross_kept, d_mem, small, own_seg, seg_row, mem_seg,
-    qkv, query, pairs_weight, out, early, conv,
+    qkv, query, pairs_weight, out, mine, across, second, conv,
 ):
     tokens, width = g1.shape
     keys, mems = row_inputs.shape[0], mem_turned.shape[1]
@@ -1438,28 +1616,27 @@
     far_count = lax.axis_size("rows") // 4
     step = 2 * far_count * LANE_GROUP
     size = width // H_CROSS
-    middle_total = conv.shape[1] + 5 * width
+    middle_total = second.shape[1] - across.shape[1] + conv.shape[1] + 5 * width
     middle_total = middle_total + -middle_total % step
     last_total = 3 * width + small.shape[0]
     last_total = last_total + -last_total % step
-    early_total = early.shape[1]
+    early_total = mine.shape[0] * step + across.shape[1]
     late = middle_total + last_total
     count = (early_total + late) // step
     slots = 3 + (seq_count - 1) + 2 * far_count
-    kept_slots = max(1, 2**19 // (seq_count * half * step))
     low, full = jnp.bfloat16, jnp.float32
     longest = max(tokens, mems)
     v = pltpu.VMEM
     in_hbm = pl.BlockSpec(memory_space=pl.ANY)
     dma = pltpu.SemaphoreType.DMA
-    d_normed, d_memory, share = pl.pallas_call(
+    grad_in, grad_mem, share = pl.pallas_call(
         closing_kernel,
         out_shape=(
-            jax.ShapeDtypeStruct((keys, width), low),
-            jax.ShapeDtypeStruct((mems, width), low),
+            jax.ShapeDtypeStruct((tokens, width), full),
+            jax.ShapeDtypeStruct((mems // seq_count, width), full),
             jax.ShapeDtypeStruct((2, half, early_total + late), low),
         ),
-        in_specs=[IN_VMEM] * 21 + [in_hbm] * 2,
+        in_specs=[IN_VMEM] * 23 + [in_hbm] * 2,
         out_specs=(IN_VMEM, IN_VMEM, in_hbm),
         scratch_shapes=[
             v((width, keys), low),
@@ -1481,20 +1658,25 @@
             v((2, longest, TILE), low),
             v((2, longest, TILE), low),
             v((seq_count, 2, half, late), low),
-            v((kept_slots, seq_count, half, step), low),
-            v((count, seq_count, half, step), low),
-            v((count, seq_count - 1, half, step), low),
+            v((late // step, seq_count, half, step), low),
+            v((late // step, seq_count - 1, half, step), low),
             v((count, half, step // 2), low),
             v((count, far_count - 1, half, LANE_GROUP), low),
             v((count, half, LANE_GROUP), low),
             dma((count, slots)),
             dma((count, slots)),
             dma((count,)),
-            dma((early_total // step,)),
-            dma(()),
+            dma((2,)),
+            v((seq_count - 1, tokens, width), low),
+            v((seq_count - 1, tokens, width), low),
+            v((tokens, width), full),
+            v((mems, width), low),
+            v((seq_count - 1, mems // seq_count, width), low),
+            dma((2, seq_count - 1)),
+            dma((2, seq_count - 1)),
         ],
         compiler_params=pltpu.CompilerParams(
-            collective_id=0, has_side_effects=True, vmem_limit_bytes=HOST_VMEM
+            collective_id=2, has_side_effects=True, vmem_limit_bytes=HOST_VMEM
         ),
         cost_estimate=pl.CostEstimate(
             flops=tokens * width * width * 200, bytes_accessed=tokens * width * 40, transcendentals=tokens * width * 20
@@ -1503,9 +1685,39 @@
     )(
         g1, row_inputs, mem_turned, gain, *self_kept, *cross_kept, d_mem, small,
         own_seg[None], seg_row[None], mem_seg[None], qkv, query, pairs_weight, out,
-        early.reshape(seq_count, 2, half, early_total), conv.reshape(seq_count, 2, half, conv.shape[1]),
-    )
-    return d_normed, d_memory, share.reshape(2 * half, early_total + late), early_total, early_total + middle_total
+        mine, across, second.reshape(seq_count, 2, half, second.shape[1]), conv.reshape(seq_count, 2, half, conv.shape[1]),
+    )
+    return grad_in, grad_mem, share.reshape(2 * half, early_total + late), early_total + middle_total
+
+
+def finishing_kernel(plan, small_at, share_ref, *outs):
+    for (offset, size, dim), out_ref in zip(plan, outs):
+        if dim == 0:
+            out_ref[...] = share_ref[:, offset : offset + size].astype(jnp.float32)
+        else:
+            for low, high in row_tiles(size, 256):
+                out_ref[low:high, :] = share_ref[:, offset + low : offset + high].astype(jnp.float32).T
+    rows = share_ref[:, small_at : small_at + 128].astype(jnp.float32).T
+    width = rows.shape[1]
+    at = 0
+    for out_ref in outs[len(plan) :]:
+        for row in range(out_ref.shape[0]):
+            for low in range(0, out_ref.shape[1], width):
+                out_ref[row : row + 1, low : low + width] = rows[at : at + 1, :]
+                at = at + 1
+
+
+def finishing(share, plan, small_at, small_shapes):
+    width = share.shape[0]
+    shapes = [(width, size) if dim == 0 else (size, width) for _, size, dim in plan] + small_shapes
+    return pl.pallas_call(
+        functools.partial(finishing_kernel, plan, small_at),
+        out_shape=tuple(jax.ShapeDtypeStruct(shape, jnp.float32) for shape in shapes),
+        in_specs=[IN_VMEM],
+        out_specs=(IN_VMEM,) * len(shapes),
+        compiler_params=pltpu.CompilerParams(vmem_limit_bytes=KERNEL_VMEM),
+        name="finishing",
+    )(share)
 
 
 def segment_reach(seg_row):
@@ -1689,7 +1901,7 @@
     down, _ = joined_weight(shards[18], 1, middle_pieces, down_at, 4)
     conv_rims = passed_along(jnp.concatenate([conv_l[:RIM], conv_r[:RIM]], 1), "seq", -1)
     more = jnp.stack(seq_rotated(normed_d))
-    result, grad_now, d_normed, d_middle, d_gains_late, d_mem = middle(
+    result, grad_now, d_normed, d_middle, d_gains_late, d_mem, across_first = middle(
         hidden_c,
         normed_d,
         more,
@@ -1706,7 +1918,7 @@
     d_hidden, g_three = norm_back(hidden_c, gain_rows[2], row_sum_owned(d_normed))
     grad_now = grad_now + d_hidden
     branch = grad_now.astype(jnp.bfloat16)
-    grad_now, d_projections, d_taps_left, d_taps_right, d_taps_mid, d_mid_gain, g_two = conv_back(
+    grad_now, d_projections, d_taps_left, d_taps_right, d_taps_mid, d_mid_gain, g_two, mine, across = conv_back(
         grad_now,
         passed_along(branch[:RIM], "seq", -1),
         conv_l,
@@ -1724,13 +1936,15 @@
         proj_left,
         proj_right,
         proj_mid,
+        across_first,
+        d_middle,
     )
     d_mid_gain, g_two = d_mid_gain[0], g_two[0]
     d_gains = jnp.concatenate([jnp.stack([jnp.zeros_like(g_two), g_two, g_three], 0), d_gains_late], 0)
     wide, narrow = proj_left.shape[1], proj_right.shape[1]
     width = model_width // lax.axis_size("seq")
     small_grads = (d_gains, d_taps_left, d_taps_right, d_mid_gain, d_taps_mid)
-    d_normed, d_memory, share, second_at, third_at = closing(
+    grad_in, grad_mem, share, last_at = closing(
         grad_now,
         row_inputs,
         mem_rows.T,
@@ -1746,34 +1960,26 @@
         query_cross,
         kv_cross,
         out_first,
+        mine,
+        across,
         d_middle,
         d_projections,
     )
-    d_hidden, _ = norm_back(inputs, gain_rows[0], row_sum_owned(d_normed))
-    grad_in = grad_now + d_hidden
-    grad_mem = row_sum_owned(d_memory)
     shares = [None] * len(shards)
     up = down.shape[0]
-    for offset, group, sizes in (
-        (
-            0,
-            (17, 18, 16, 14, 15, 12, 13),
-            (up, up, model_width, model_width, 2 * model_width, 3 * model_width, model_width),
-        ),
-        (
-            second_at,
-            (11, 6, 8, 4, 3, 2),
-            (wide, wide, narrow, 2 * model_width, 2 * model_width, model_width),
-        ),
-        (third_at, (1,), (3 * model_width,)),
+    plan, order, offset = [], (17, 18, 16, 14, 15, 12, 13, 11, 6, 8, 4, 3, 2, 1), 0
+    for k, size in zip(
+        order,
+        (up, up, model_width, model_width, 2 * model_width, 3 * model_width, model_width)
+        + (wide, wide, narrow, 2 * model_width, 2 * model_width, model_width, 3 * model_width),
     ):
-        for k, size in zip(group, sizes):
-            piece = share[:, offset : offset + size].astype(jnp.float32)
-            shares[k] = piece if shard_dims[k] == 0 else piece.T
-            offset = offset + size
-    parts = small_shares(share[:, offset : offset + 128].astype(jnp.float32), small_grads, width)
-    for k, piece in zip(small, parts):
-        shares[k] = piece
+        offset = last_at if k == 1 else offset
+        plan.append((offset, size, shard_dims[k]))
+        offset = offset + size
+    small_shapes = [shards[k].shape if k != 9 else (1, shards[k].shape[0]) for k in small]
+    found = finishing(share, plan, offset, small_shapes)
+    for k, piece in zip(order + small, found):
+        shares[k] = piece.reshape(shards[k].shape)
     return (
         result[None],
         grad_in[None],

time: 455 us -> 421 us (0.925)
  other arithmetic: 50.8 us -> 24.4 us
  Pallas kernels: 244 us -> 264 us
  starting transfers between devices: 38.8 us -> 20.7 us
  local copies, waits for them, and re-layouts: 54.4 us -> 46.3 us
    ppermute x3 -> x1, starting transfers between devices: 20.2 us -> 1.61 us  [halved_sum(): lax.ppermute(sent, axis, [(i, i ^ bit) for i in range(lax.axis_size(axis))])]
    pallas_call x1, Pallas kernels: 56.5 us -> 71.9 us  [middle(): pl.pallas_call(functools.partial(middle_kernel, len(pieces)), out_shape=(...]
    convert_element_type x4 -> x0, other arithmetic: 11.5 us -> none  [local(): piece = share[:, offset:offset + size].astype(jnp.float32)]
    pallas_call x1, Pallas kernels: 27.6 us -> 36.4 us  [conv_back(): pl.pallas_call(conv_bwd_kernel, out_shape=(jax.ShapeDtypeStruct((tokens,...]
    pallas_call x1 -> x2, Pallas kernels: 131 us -> 126 us  [the longest x1 117 us: closing(): pl.pallas_call(closing_kernel, out_shape=(jax.ShapeDtypeStruct((tokens, w...]
    unnamed x145 -> x157, local copies, waits for them, and re-layouts: 24.7 us -> 21.7 us
    ppermute x3 -> x1, waiting for transfers between devices: 13.4 us -> 13 us  [halved_sum(): lax.ppermute(sent, axis, [(i, i ^ bit) for i in range(lax.axis_size(axis))])]
  transfers between devices with their start and end apart: 20 -> 18, of which waited for: 9 -> 8; matrix products, arithmetic and copies ran while one was open for 17% -> 12% of each run, Pallas kernels for 7% -> 7%
where the time goes in v1:
time: 421 us; the launch traced here: 413 us
  Pallas kernels  264 us (63%)
  waiting for transfers between devices  48.6 us (12%)
  local copies, waits for them, and re-layouts  46.3 us (11%)
  other arithmetic  24.4 us (6%)
  starting transfers between devices  20.7 us (5%)
  matrix products  4.95 us (1%)
    pallas_call x1, Pallas kernels, closing(): pl.pallas_call(closing_kernel, out_shape=(jax.ShapeDtypeStruct((tokens, w...  117 us
    pallas_call x1, Pallas kernels, middle(): pl.pallas_call(functools.partial(middle_kernel, len(pieces)), out_shape=(...  71.9 us
    pallas_call x1, Pallas kernels, conv_back(): pl.pallas_call(conv_bwd_kernel, out_shape=(jax.ShapeDtypeStruct((tokens,...  36.4 us
    ppermute x8, waiting for transfers between devices, rotated(): lax.ppermute(block, axis, [((i + distance) % size, i) for i in range(size)])  28.1 us
    unnamed x157, local copies, waits for them, and re-layouts  21.7 us
    pallas_call x1, Pallas kernels, conv_forward(): pl.pallas_call(conv_fwd_kernel, out_shape=(jax.ShapeDtypeStruct((tokens,...  17.1 us
    ppermute x1, waiting for transfers between devices, halved_sum(): lax.ppermute(sent, axis, [(i, i ^ bit) for i in range(lax.axis_size(axis))])  13 us
    pallas_call x2, Pallas kernels, attend_forward(): pl.pallas_call(functools.partial(attend_kernel, heads, causal), out_shape...  12.5 us
  transfers between devices with their start and end apart: 18, of which 8 were waited for; matrix products, arithmetic and copies ran while one was open for 12% of the time, Pallas kernels for 7%

profile of v1, /device:TPU:0, one launch (start us, length us, event | category | flops | bytes accessed | tf_op | source)
XLA Modules:
  0.0 412.7 jit_solution(8595240411406001324)
XLA Ops:
  5.6 3.0 collective-permute-start.2
  9.8 2.0 collective-permute-start.4
  16.2 1.6 dynamic-slice_dynamic-update-slice_fusion.1
  21.5 1.5 dynamic-slice_dynamic-update-slice_fusion.5
  23.0 1.5 dynamic-slice_dynamic-update-slice_fusion.4
  24.5 1.6 dynamic-slice_dynamic-update-slice_fusion.2
  26.0 1.5 dynamic-slice_dynamic-update-slice_fusion.3
  27.6 1.7 dynamic-slice_dynamic-update-slice_fusion
  33.5 2.0 collective-permute-start.3
  35.5 4.2 %collective-permute-done.7 = bf16[128,512]{0,1:T(8,128)(2,1)S(1)} collective-permute-done((bf16[128,512]{0,1:T(8,128)(2,1)S(1)}, bf16[128,512]{0,1:T(8,128)(2,1)S(1)}, u32[]{:S(2)}, u32[]{:S(2)}) %collective-permute-start.7) | collective-permute-done | bytes 131104 | tf_op jit(solution)/shard_map/ppermute | solution.py:24
  39.9 1.8 convert_reduce_fusion
  44.5 2.1 convolution_convert_fusion.refs_1_.paira_ref
  46.7 5.1 %collective-permute-done.3 = bf16[128,2560]{1,0:T(8,128)(2,1)S(1)} collective-permute-done((bf16[128,2560]{1,0:T(8,128)(2,1)}, bf16[128,2560]{1,0:T(8,128)(2,1)S(1)}, u32[]{:S(2)}, u32[]{:S(2)}) %collective-permute-start.3) | collective-permute-done | bytes 655392 | tf_op jit(solution)/shard_map/ppermute | solution.py:24
  54.9 9.1 %attend_fwd.2 = (bf16[512,640]{1,0:T(8,128)(2,1)S(1)}, f32[16,1,640]{2,1,0:T(1,128)S(1)}) custom-call(s32[1]{0:T(128)} %bitcast.1.place_ref, bf16[512,640]{1,0:T(8,128)(2,1)S(1)} %convolution_convert_fusion.2.refs_0_.qa_ref, bf16[1024,1280]{1,0:T(8,128)(2,1)S(1)} %convolution_convert_fusion.refs_1_.paira_ref, ...), custom_call_target="tpu_custom_call" | custom-call | flops 7864320000 | bytes 2621440 | tf_op jit(solution)/shard_map/attend_fwd/pallas_call | solution.py:502
  64.1 1.6 collective-permute-start.8
  69.2 3.4 attend_fwd.3
  77.6 7.1 %collective-permute-done.9.rest_0_ = bf16[64,8192]{1,0:T(8,128)(2,1)} collective-permute-done((bf16[64,8192]{1,0:T(8,128)(2,1)S(1)}, bf16[64,8192]{1,0:T(8,128)(2,1)}, u32[]{:S(2)}, u32[]{:S(2)}) %collective-permute-start.9) | collective-permute-done | bytes 1048608 | tf_op jit(solution)/shard_map/ppermute | solution.py:24
  85.6 5.1 %collective-permute-start.10 = (bf16[16,512]{1,0:T(8,128)(2,1)S(1)}, bf16[16,512]{1,0:T(8,128)(2,1)S(1)}, u32[]{:S(2)}, u32[]{:S(2)}) collective-permute-start(bf16[16,512]{1,0:T(8,128)(2,1)S(1)} %slice.212), channel_id=1, source_target_pairs={{0,1},{2,3},{4,5},{6,7},{8,9},{10,11},{12,13},{14,15},{16,17},{18,... | collective-permute-start | bytes 49160 | tf_op jit(solution)/shard_map/ppermute | solution.py:182
  96.3 17.1 %conv_fwd.1 = (bf16[640,512]{1,0:T(8,128)(2,1)S(1)}, bf16[640,512]{1,0:T(8,128)(2,1)S(1)}, bf16[640,1024]{1,0:T(8,128)(2,1)}, f32[640,512]{1,0:T(8,128)}, bf16[640,512]{1,0:T(8,128)(2,1)S(1)}) custom-call(f32[640,512]{1,0:T(8,128)} %copy-done.22, bf16[640,512]{1,0:T(8,128)(2,1)S(1)} %multiply_convert_fusion.a2_ref, ...), custom_call_target="tpu_custom_call" | custom-call | flops 6710886400 | bytes 5242880 | tf_op jit(solution)/shard_map/conv_fwd/pallas_call | solution.py:681
  113.4 2.9 collective-permute-done.12.rest_1_
  117.3 2.8 pad_maximum_fusion
  127.2 1.9 maximum_select_fusion.down_ref
  129.1 11.6 %collective-permute-done.13 = bf16[640,512]{1,0:T(8,128)(2,1)S(1)} collective-permute-done((bf16[640,512]{1,0:T(8,128)(2,1)S(1)}, bf16[640,512]{1,0:T(8,128)(2,1)S(1)}, u32[]{:S(2)}, u32[]{:S(2)}) %collective-permute-start.13) | collective-permute-done | bytes 655392 | tf_op jit(solution)/shard_map/ppermute | solution.py:24
  141.6 71.9 %middle.1 = (bf16[640,512]{1,0:T(8,128)(2,1)}, f32[640,512]{1,0:T(8,128)}, bf16[1280,512]{1,0:T(8,128)(2,1)}, bf16[512,4096]{1,0:T(8,128)(2,1)}, f32[2,512]{1,0:...) custom-call(f32[640,512]{1,0:T(8,128)} %get-tuple-element.98.h2_ref, bf16[640,512]{1,0:T(8,128)(2,1)} %copy-done.14, ...), custom_call_target="tpu_custom_call" | custom-call | flops 33554432000 | bytes 13107200 | tf_op jit(solution)/shard_map/middle/pallas_call | solution.py:1129
  214.7 1.6 collective-permute-start.15
  218.1 13.0 %collective-permute-done.15 = bf16[640,512]{1,0:T(8,128)(2,1)} collective-permute-done((bf16[640,512]{1,0:T(8,128)(2,1)S(1)}, bf16[640,512]{1,0:T(8,128)(2,1)}, u32[]{:S(2)}, u32[]{:S(2)}) %collective-permute-start.15) | collective-permute-done | bytes 655392 | tf_op jit(solution)/shard_map/ppermute | solution.py:163
  231.1 1.9 fusion.18
  236.5 3.7 collective-permute-done.16.brim_ref
  240.8 36.4 %conv_bwd.1 = (f32[640,512]{1,0:T(8,128)}, bf16[512,2304]{1,0:T(8,128)(2,1)}, f32[11,512]{1,0:T(8,128)}, f32[7,512]{1,0:T(8,128)}, f32[7,1024]{1,0:T(8,128)}, /*...) custom-call(f32[640,512]{1,0:T(8,128)} %copy-done.31, ...), custom_call_target="tpu_custom_call" | custom-call | flops 13421772800 | bytes 13107200 | tf_op jit(solution)/shard_map/conv_bwd/pallas_call | solution.py:883
  280.0 2.5 concatenate.299
  283.2 116.7 %closing.1 = (f32[640,512]{1,0:T(8,128)}, f32[128,512]{1,0:T(8,128)}, bf16[2,128,15360]{2,1,0:T(8,128)(2,1)}) custom-call(f32[640,512]{1,0:T(8,128)} %get-tuple-element.111.g1_ref, bf16[1280,512]{1,0:T(8,128)(2,1)} %copy-done.25, bf16[512,256]{1,0:T(8,128)(2,1)} %bitcast.144, f32[1,512]{1,0:T(1,128)} %copy-done.63, bf16[512,640]{1,0:T(8,128)(2,1)} %copy-done.3, ...), custom_call_target="tpu_custom_call" | custom-call | flops 33554432000 | bytes 13107200 | tf_op jit(solution)/shard_map/closing/pallas_call | solution.py:1632
  399.9 9.0 %finishing.1 = (f32[256,2048]{1,0:T(8,128)}, f32[2048,256]{1,0:T(8,128)}, f32[256,512]{1,0:T(8,128)}, f32[256,512]{1,0:T(8,128)}, f32[256,1024]{1,0:T(8,128)}, /...) custom-call(bf16[256,15360]{1,0:T(8,128)(2,1)} %bitcast.136), custom_call_target="tpu_custom_call" | custom-call | tf_op jit(solution)/shard_map/finishing/pallas_call | solution.py:1713
  (310 shorter events, 59.8 us)
Async XLA Ops:
  0.7 12.8 %copy-start.37 = (bf16[1024,256]{1,0:T(8,128)(2,1)S(1)}, bf16[1024,256]{1,0:T(8,128)(2,1)}, u32[]{:S(2)}) copy-start(bf16[1024,256]{1,0:T(8,128)(2,1)} %param.33) | copy-start | bytes 1572868
  5.6 26.4 %collective-permute-start.2 = (bf16[80,128]{1,0:T(8,128)(2,1)S(1)}, bf16[80,128]{1,0:T(8,128)(2,1)S(1)}, u32[]{:S(2)}, u32[]{:S(2)}) collective-permute-start(bf16[80,128]{1,0:T(8,128)(2,1)S(1)} %pad_bitcast_fusion), channel_id=1, source_target_pairs={{1,0},{0,1},{3,2},{2,3},{5,4},{4,5},{7,6},{6,7},{9,8},{8,9},{11,10... | collective-permute-start | bytes 61448 | tf_op jit(solution)/shard_map/ppermute | solution.py:24
  9.7 23.7 %collective-permute-start = (bf16[128,1536]{1,0:T(8,128)(2,1)S(1)}, bf16[128,1536]{1,0:T(8,128)(2,1)}, u32[]{:S(2)}, u32[]{:S(2)}) collective-permute-start(bf16[128,1536]{1,0:T(8,128)(2,1)S(1)} %constant_dynamic-slice_fusion.9), channel_id=1, source_target_pairs={{1,0},{0,1},{3,2},{2,3},{5,4},{4,5},{7,6},{6,7},{9,8},{8,9},{11,10... | collective-permute-start | bytes 1179656 | tf_op jit(solution)/shard_map/ppermute | solution.py:24
  9.8 30.1 %collective-permute-start.4 = (bf16[640,512]{1,0:T(8,128)(2,1)}, bf16[640,512]{1,0:T(8,128)(2,1)}, u32[]{:S(2)}, u32[]{:S(2)}) collective-permute-start(bf16[640,512]{1,0:T(8,128)(2,1)} %bitcast.134), channel_id=1, source_target_pairs={{1,0},{0,1},{3,2},{2,3},{5,4},{4,5},{7,6},{6,7},{9,8},{8,9},{11,10... | collective-permute-start | bytes 1966088 | tf_op jit(solution)/shard_map/ppermute | solution.py:24
  31.6 37.3 %copy-start.11 = (s32[1,640]{1,0:T(1,128)}, s32[1,640]{1,0:T(1,128)S(1)}, u32[]{:S(2)}) copy-start(s32[1,640]{1,0:T(1,128)S(1)} %constant_dynamic-slice_fusion.5.refs_2_.qseg_ref) | copy-start | bytes 7684
  32.0 53.2 %copy-start.64 = (f32[1,512]{1,0:T(1,128)}, f32[1,512]{1,0:T(1,128)S(1)}, u32[]{:S(2)}) copy-start(f32[1,512]{1,0:T(1,128)S(1)} %get-tuple-element.175.gain_ref) | copy-start | bytes 6148
  32.1 64.1 %copy-start.6 = (f32[11,512]{1,0:T(8,128)}, f32[11,512]{1,0:T(8,128)S(1)}, u32[]{:S(2)}) copy-start(f32[11,512]{1,0:T(8,128)S(1)} %fusion.28.tl_ref) | copy-start | bytes 67588
  32.2 64.1 %copy-start.9 = (f32[7,512]{1,0:T(8,128)}, f32[7,512]{1,0:T(8,128)S(1)}, u32[]{:S(2)}) copy-start(f32[7,512]{1,0:T(8,128)S(1)} %fusion.31.tr_ref) | copy-start | bytes 43012
  33.3 6.4 %collective-permute-start.7 = (bf16[128,512]{0,1:T(8,128)(2,1)S(1)}, bf16[128,512]{0,1:T(8,128)(2,1)S(1)}, u32[]{:S(2)}, u32[]{:S(2)}) collective-permute-start(bf16[128,512]{0,1:T(8,128)(2,1)S(1)} %bitcast.157), channel_id=1, source_target_pairs={{1,0},{0,1},{3,2},{2,3},{5,4},{4,5},{7,6},{6,7},{9,8},{8,9},{11,10... | collective-permute-start | bytes 393224 | tf_op jit(solution)/shard_map/ppermute | solution.py:24
  33.4 62.8 %copy-start.10 = (f32[1,1024]{1,0:T(1,128)}, f32[1,1024]{1,0:T(1,128)S(1)}, u32[]{:S(2)}) copy-start(f32[1,1024]{1,0:T(1,128)S(1)} %fusion.32.mgain_ref) | copy-start | bytes 12292
  33.5 62.7 %copy-start.7 = (f32[7,1024]{1,0:T(8,128)}, f32[7,1024]{1,0:T(8,128)S(1)}, u32[]{:S(2)}) copy-start(f32[7,1024]{1,0:T(8,128)S(1)} %fusion.29.tm_ref) | copy-start | bytes 86020
  33.5 18.3 %collective-permute-start.3 = (bf16[128,2560]{1,0:T(8,128)(2,1)}, bf16[128,2560]{1,0:T(8,128)(2,1)S(1)}, u32[]{:S(2)}, u32[]{:S(2)}) collective-permute-start(bf16[128,2560]{1,0:T(8,128)(2,1)} %pad_maximum_fusion.1), channel_id=1, source_target_pairs={{1,0},{0,1},{3,2},{2,3},{5,4},{4,5},{7,6},{6,7},{9,8},{8,9},{11,10... | collective-permute-start | bytes 1966088 | tf_op jit(solution)/shard_map/ppermute | solution.py:24
  35.5 6.9 %collective-permute-start.1 = (bf16[128,1536]{1,0:T(8,128)(2,1)}, bf16[128,1536]{1,0:T(8,128)(2,1)S(1)}, u32[]{:S(2)}, u32[]{:S(2)}) collective-permute-start(bf16[128,1536]{1,0:T(8,128)(2,1)} %collective-permute-done), channel_id=1, source_target_pairs={{0,2},{2,0},{4,6},{6,4},{8,10},{10,8},{12,14},{14,12},{16,18},{18,... | collective-permute-start | bytes 1179656 | tf_op jit(solution)/shard_map/ppermute | solution.py:28
  39.9 28.6 %copy-start.41 = (bf16[256,512]{0,1:T(8,128)(2,1)}, bf16[256,512]{0,1:T(8,128)(2,1)S(1)}, u32[]{:S(2)}) copy-start(bf16[256,512]{0,1:T(8,128)(2,1)S(1)} %maximum_select_fusion.17) | copy-start | bytes 786436
  51.8 12.3 %collective-permute-start.5 = (bf16[128,2560]{1,0:T(8,128)(2,1)S(1)}, bf16[128,2560]{1,0:T(8,128)(2,1)S(1)}, u32[]{:S(2)}, u32[]{:S(2)}) collective-permute-start(bf16[128,2560]{1,0:T(8,128)(2,1)S(1)} %collective-permute-done.3), channel_id=1, source_target_pairs={{0,2},{2,0},{4,6},{6,4},{8,10},{10,8},{12,14},{14,12},{16,18},{18,... | collective-permute-start | bytes 1966088 | tf_op jit(solution)/shard_map/ppermute | solution.py:28
  52.8 11.3 %collective-permute-start.6 = (bf16[64,2304]{1,0:T(8,128)(2,1)S(1)}, bf16[64,2304]{1,0:T(8,128)(2,1)S(1)}, u32[]{:S(2)}, u32[]{:S(2)}) collective-permute-start(bf16[64,2304]{1,0:T(8,128)(2,1)S(1)} %copy-done.54), channel_id=1, source_target_pairs={{1,0},{0,1},{3,2},{2,3},{5,4},{4,5},{7,6},{6,7},{9,8},{8,9},{11,10... | collective-permute-start | bytes 884744 | tf_op jit(solution)/shard_map/ppermute | solution.py:24
  53.5 31.3 %collective-permute-start.9 = (bf16[64,8192]{1,0:T(8,128)(2,1)S(1)}, bf16[64,8192]{1,0:T(8,128)(2,1)}, u32[]{:S(2)}, u32[]{:S(2)}) collective-permute-start(bf16[64,8192]{1,0:T(8,128)(2,1)S(1)} %copy-done.58), channel_id=1, source_target_pairs={{1,0},{0,1},{3,2},{2,3},{5,4},{4,5},{7,6},{6,7},{9,8},{8,9},{11,10... | collective-permute-start | bytes 3145736 | tf_op jit(solution)/shard_map/ppermute | solution.py:24
  64.0 13.0 %copy-start.3 = (bf16[512,640]{1,0:T(8,128)(2,1)}, bf16[512,640]{1,0:T(8,128)(2,1)S(1)}, u32[]{:S(2)}) copy-start(bf16[512,640]{1,0:T(8,128)(2,1)S(1)} %get-tuple-element.89.atta_ref) | copy-start | bytes 1966084
  64.1 10.1 %collective-permute-start.8 = (bf16[64,2304]{1,0:T(8,128)(2,1)S(1)}, bf16[64,2304]{1,0:T(8,128)(2,1)S(1)}, u32[]{:S(2)}, u32[]{:S(2)}) collective-permute-start(bf16[64,2304]{1,0:T(8,128)(2,1)S(1)} %collective-permute-done.6), channel_id=1, source_target_pairs={{0,4},{2,6},{4,0},{6,2},{8,12},{10,14},{12,8},{14,10},{16,20},{18,... | collective-permute-start | bytes 884744 | tf_op jit(solution)/shard_map/ppermute | solution.py:50
  75.2 16.1 %collective-permute-start.11 = (bf16[128,2304]{1,0:T(8,128)(2,1)}, bf16[128,2304]{1,0:T(8,128)(2,1)}, u32[]{:S(2)}, u32[]{:S(2)}) collective-permute-start(bf16[128,2304]{1,0:T(8,128)(2,1)} %pad_maximum_fusion.2), channel_id=1, source_target_pairs={{0,2},{2,0},{4,6},{6,4},{8,10},{10,8},{12,14},{14,12},{16,18},{18,... | collective-permute-start | bytes 1769480 | tf_op jit(solution)/shard_map/ppermute | solution.py:28
  85.6 10.6 %collective-permute-start.10 = (bf16[16,512]{1,0:T(8,128)(2,1)S(1)}, bf16[16,512]{1,0:T(8,128)(2,1)S(1)}, u32[]{:S(2)}, u32[]{:S(2)}) collective-permute-start(bf16[16,512]{1,0:T(8,128)(2,1)S(1)} %slice.212), channel_id=1, source_target_pairs={{0,1},{2,3},{4,5},{6,7},{8,9},{10,11},{12,13},{14,15},{16,17},{18,... | collective-permute-start | bytes 49160 | tf_op jit(solution)/shard_map/ppermute | solution.py:182
  90.7 25.6 %collective-permute-start.12 = (bf16[64,8192]{1,0:T(8,128)(2,1)}, bf16[64,8192]{1,0:T(8,128)(2,1)S(1)}, u32[]{:S(2)}, u32[]{:S(2)}) collective-permute-start(bf16[64,8192]{1,0:T(8,128)(2,1)} %collective-permute-done.9.rest_0_), channel_id=1, source_target_pairs={{0,4},{2,6},{4,0},{6,2},{8,12},{10,14},{12,8},{14,10},{16,20},{18,... | collective-permute-start | bytes 3145736 | tf_op jit(solution)/shard_map/ppermute | solution.py:50
  95.0 18.4 %copy-start = (bf16[512,1024]{1,0:T(8,128)(2,1)}, bf16[512,1024]{1,0:T(8,128)(2,1)S(1)}, u32[]{:S(2)}) copy-start(bf16[512,1024]{1,0:T(8,128)(2,1)S(1)} %maximum_select_fusion.5.pl_ref) | copy-start | bytes 3145732
  96.1 17.3 %copy-start.1 = (bf16[1024,512]{1,0:T(8,128)(2,1)}, bf16[1024,512]{1,0:T(8,128)(2,1)S(1)}, u32[]{:S(2)}) copy-start(bf16[1024,512]{1,0:T(8,128)(2,1)S(1)} %maximum_select_fusion.6.pm_ref) | copy-start | bytes 3145732
  96.2 17.2 %copy-start.5 = (bf16[512,256]{1,0:T(8,128)(2,1)}, bf16[512,256]{1,0:T(8,128)(2,1)S(1)}, u32[]{:S(2)}) copy-start(bf16[512,256]{1,0:T(8,128)(2,1)S(1)} %maximum_select_fusion.20.pr_ref) | copy-start | bytes 786436
  120.0 4.5 %collective-permute-start.14 = (bf16[128,8192]{1,0:T(8,128)(2,1)}, bf16[128,8192]{1,0:T(8,128)(2,1)}, u32[]{:S(2)}, u32[]{:S(2)}) collective-permute-start(bf16[128,8192]{1,0:T(8,128)(2,1)} %pad_maximum_fusion), channel_id=1, source_target_pairs={{0,2},{2,0},{4,6},{6,4},{8,10},{10,8},{12,14},{14,12},{16,18},{18,... | collective-permute-start | bytes 6291464 | tf_op jit(solution)/shard_map/ppermute | solution.py:28
  123.5 17.2 %collective-permute-start.13 = (bf16[640,512]{1,0:T(8,128)(2,1)S(1)}, bf16[640,512]{1,0:T(8,128)(2,1)S(1)}, u32[]{:S(2)}, u32[]{:S(2)}) collective-permute-start(bf16[640,512]{1,0:T(8,128)(2,1)S(1)} %get-tuple-element.101.a3_ref), channel_id=1, source_target_pairs={{1,0},{0,1},{3,2},{2,3},{5,4},{4,5},{7,6},{6,7},{9,8},{8,9},{11,10... | collective-permute-start | bytes 1966088 | tf_op jit(solution)/shard_map/ppermute | solution.py:24
  214.7 16.4 %copy-start.33 = (bf16[1280,512]{1,0:T(8,128)(2,1)S(1)}, bf16[1280,512]{1,0:T(8,128)(2,1)}, u32[]{:S(2)}) copy-start(bf16[1280,512]{1,0:T(8,128)(2,1)} %get-tuple-element.105) | copy-start | bytes 3932164
  214.7 16.4 %collective-permute-start.15 = (bf16[640,512]{1,0:T(8,128)(2,1)S(1)}, bf16[640,512]{1,0:T(8,128)(2,1)}, u32[]{:S(2)}, u32[]{:S(2)}) collective-permute-start(bf16[640,512]{1,0:T(8,128)(2,1)S(1)} %constant_dynamic-slice_fusion), channel_id=1, source_target_pairs={{0,1},{1,0},{2,3},{3,2},{4,5},{5,4},{6,7},{7,6},{8,9},{9,8},{10,11... | collective-permute-start | bytes 1966088 | tf_op jit(solution)/shard_map/ppermute | solution.py:163
  216.5 19.4 %collective-permute-start.17 = (bf16[16,1024]{1,0:T(8,128)(2,1)S(1)}, bf16[16,1024]{1,0:T(8,128)(2,1)S(1)}, u32[]{:S(2)}, u32[]{:S(2)}) collective-permute-start(bf16[16,1024]{1,0:T(8,128)(2,1)S(1)} %pad_maximum_fusion.4), channel_id=1, source_target_pairs={{1,0},{3,2},{5,4},{7,6},{9,8},{11,10},{13,12},{15,14},{17,16},{19,... | collective-permute-start | bytes 98312 | tf_op jit(solution)/shard_map/ppermute | solution.py:182
  234.6 5.6 %collective-permute-start.16 = (bf16[16,512]{1,0:T(8,128)(2,1)S(1)}, bf16[16,512]{1,0:T(8,128)(2,1)S(1)}, u32[]{:S(2)}, u32[]{:S(2)}) collective-permute-start(bf16[16,512]{1,0:T(8,128)(2,1)S(1)} %slice.240), channel_id=1, source_target_pairs={{1,0},{3,2},{5,4},{7,6},{9,8},{11,10},{13,12},{15,14},{17,16},{19,... | collective-permute-start | bytes 49160 | tf_op jit(solution)/shard_map/ppermute | solution.py:182
  240.8 39.2 %copy-start.65 = (f32[2,512]{1,0:T(2,128)S(1)}, f32[2,512]{1,0:T(2,128)}, u32[]{:S(2)}) copy-start(f32[2,512]{1,0:T(2,128)} %get-tuple-element.116) | copy-start | bytes 12292
  (57 other events, 250.5 us)
